TPU v7x, 256 devices: a whole 4x4x8 slice. The times are simulated.
256 devices in a mesh: pop: 32 (over z, y), wa: 8 (over x, core).
Axes of the slice: x: 4, y: 4, z: 8, core: 2. Of those that a mesh axis runs over, the one named last changes fastest.
Arguments:
- inputs: bfloat16 [16384, 4096], P('pop'), may hold values from -6 to 6
- noise_left: bfloat16 [16384, 4096], P('pop'), may hold values from -6 to 6
- noise_right: bfloat16 [16384, 8192], P('pop', 'wa'), may hold values from -6 to 6
- reward_probe: float32 [8192], P('wa'), may hold values from -6 to 6
- scores: int32 [16384], P('pop'), may hold values from 0 to 31
- master: float32 [4096, 8192], P('pop', 'wa'), may hold values from -0.1 to 0.1, as said below
Outputs:
- fitness: float32 [16384], P('pop')
- update: float32 [4096, 8192], P('pop', 'wa')
- new_master: float32 [4096, 8192], P('pop', 'wa')
- new_copy: bfloat16 [4096, 8192], P('pop', 'wa')
Inputs may be any that keep to these rules, and one draw needn't show every extreme that they name: master's entries are values that bfloat16 represents exactly.
All inputs are finite; a program needn't handle non-finite values.
Results may differ from a plain program's by a relative error of at most 0.0037.
Values may be sent and summed in bfloat16 or wider, within the bound.
No kernel may reach another device: no remote copies, remote signals or barrier semaphores. Data moves between devices by JAX's collectives and lax.ppermute only.
A program may use at most 128 MiB of HBM per device.

v0:
```python
import math

import jax
import jax.numpy as jnp
from jax import lax
from jax.sharding import PartitionSpec as P

D = 4096
F = 8192


noise_scale = 0.5
learn_rate = 0.01
epsilon = 1e-05


def shards(inputs, noise_left, noise_right, reward_probe, scores, master):
    members = inputs.shape[0]
    population = members * lax.axis_size("pop")
    weight_half = master.astype(jnp.bfloat16)
    base_out = jnp.dot(
        inputs,
        lax.all_gather(weight_half, "pop", axis=0, tiled=True),
        preferred_element_type=jnp.float32,
    )
    projected = jnp.sum(
        inputs.astype(jnp.float32) * noise_left.astype(jnp.float32), axis=1
    ) / math.sqrt(D)
    outputs = base_out + noise_scale * projected[:, None] * noise_right.astype(jnp.float32)
    partial_value = jnp.dot(
        jnp.tanh(outputs), reward_probe, precision=lax.Precision.HIGHEST
    ) / math.sqrt(F)
    reward = lax.psum(partial_value, "wa")
    raw_fitness = reward + scores.astype(jnp.float32) / 16.0
    first_sum, second_sum = lax.psum(
        (jnp.sum(raw_fitness), jnp.sum(raw_fitness * raw_fitness)), "pop"
    )
    center = first_sum / population
    spread = second_sum / population - center * center
    fitness = (raw_fitness - center) * lax.rsqrt(spread + epsilon)
    scaled = ((fitness / math.sqrt(population))[:, None] * noise_right.astype(jnp.float32)).astype(
        jnp.bfloat16
    )
    dims = (((0,), (0,)), ((), ()))
    update = lax.psum_scatter(
        lax.dot_general(noise_left, scaled, dims, preferred_element_type=jnp.float32),
        "pop",
        scatter_dimension=0,
        tiled=True,
    )
    new_master = master + learn_rate * update
    return (fitness, update, new_master, new_master.astype(jnp.bfloat16))


def solution(mesh):
    return jax.shard_map(
        shards,
        mesh=mesh,
        in_specs=(
            P("pop", None),
            P("pop", None),
            P("pop", "wa"),
            P("wa"),
            P("pop"),
            P("pop", "wa"),
        ),
        out_specs=(P("pop"), P("pop", "wa"), P("pop", "wa"), P("pop", "wa")),
        check_vma=False,
    )
```

profile of v0, /device:TPU:16, one launch (start us, length us, event | category | flops | bytes accessed | tf_op | source)
XLA Modules:
  0.0 475.2 jit_solution(4833617432571927806)
XLA Ops:
  7.2 0.0 copy-start
  7.2 0.0 all-gather.2.cloned.1.call-start
  7.2 1.8 convert_element_type.22
  9.0 0.0 all-gather.2.cloned.1.call-update
  9.0 0.0 reduce-scatter.2.cloned.1.call-start
  9.1 4.6 multiply_reduce_fusion
  13.7 0.0 copy-start.2
  13.7 0.0 copy-start.3
  13.7 97.2 %all-gather.2.cloned.1.call-done = bf16[4096,1024]{1,0:T(8,128)(2,1)} async-done(((bf16[128,1024]{1,0:T(8,128)(2,1)}), bf16[4096,1024]{1,0:T(8,128)(2,1)}) %all-gather.2.cloned.1.call-update) | async-done | bytes 8388624 | tf_op jit(solution)/shard_map/all_gather | solution.py:23
  111.0 8.1 %fusion.10 = f32[512,1024]{1,0:T(8,128)S(1)} fusion(bf16[512,4096]{1,0:T(8,128)(2,1)} %param.6, bf16[4096,1024]{1,0:T(8,128)(2,1)} %all-gather.2.cloned.1.call-done), kind=kOutput, calls=%fused_computation.19 | convolution fusion | flops 4294967296 | bytes 14680064 | tf_op jit(solution)/shard_map/dot_general | solution.py:21
  119.1 0.0 copy-done
  119.1 0.0 copy-done.2
  119.1 2.2 fusion.2
  121.3 14.1 %psum.21 = f32[512]{0:T(512)S(1)} all-reduce(f32[512]{0:T(512)S(1)} %broadcast_multiply_fusion), channel_id=1, replica_groups=mesh['pop'=32,'wa'=8] {'wa'}, use_global_device_ids=true, to_apply=%region_1.0 | all-reduce | flops 512 | bytes 4096 | tf_op jit(solution)/shard_map/psum | solution.py:33
  135.5 0.0 copy-done.3
  135.5 0.6 fusion.8
  136.1 69.2 %all-reduce = (f32[]{:T(128)}, f32[]{:T(128)}) all-reduce(f32[]{:T(128)} %get-tuple-element.9, f32[]{:T(128)} %get-tuple-element.8), channel_id=1, replica_groups=mesh['pop'=32,'wa'=8] {'pop'}, use_global_device_ids=true, to_apply=%region_5.0 | all-reduce | flops 2 | bytes 16 | tf_op jit(solution)/shard_map/psum | solution.py:35
  207.9 0.6 broadcast_multiply_fusion.1
  208.5 10.4 %convolution_bitcast_fusion = f32[4096,1024]{0,1:T(8,128)} fusion(bf16[512,4096]{1,0:T(8,128)(2,1)} %param.7, bf16[512,1024]{1,0:T(8,128)(2,1)S(1)} %copy-done.2, f32[512]{0:T(512)S(1)} %get-tuple-element.14), kind=kOutput, calls=%fused_computation | convolution fusion | flops 4296540160 | bytes 22022144 | tf_op jit(solution)/shard_map/dot_general | solution.py:46
  218.9 0.0 copy-start.1
  218.9 0.0 reduce-scatter.2.cloned.1.call-update
  218.9 1.0 copy-done.1
  219.9 0.2 copy.10
  220.1 243.2 %reduce-scatter.2.cloned.1.call-done = f32[128,1024]{0,1:T(8,128)} async-done(((f32[4096,1024]{0,1:T(8,128)}), f32[128,1024]{0,1:T(8,128)}) %reduce-scatter.2.cloned.1.call-update) | async-done | bytes 524304 | tf_op jit(solution)/shard_map/reduce_scatter | solution.py:45
  463.3 1.2 fusion.9
  464.5 1.0 copy.12
  465.5 0.9 copy.13
  466.3 2.0 copy.11
  (2 shorter events, 0.0 us)
Async XLA Ops:
  7.2 112.0 %copy-start = (f32[1024]{0:T(1024)S(1)}, f32[1024]{0:T(1024)}, u32[]{:S(2)}) copy-start(f32[1024]{0:T(1024)} %param.9) | copy-start | bytes 12292
  7.2 103.8 %all-gather.2.cloned.1.call-start = ((), (), s32[]{:S(2)}) async-start(), calls=%async_computation.1 | async-start | bytes 8650752 | tf_op jit(solution)/shard_map/all_gather | solution.py:23
  9.0 454.3 %reduce-scatter.2.cloned.1.call-start = ((), (), s32[]{:S(2)}) async-start(), calls=%async_computation.2 | async-start | bytes 17301504 | tf_op jit(solution)/shard_map/reduce_scatter | solution.py:45
  13.7 105.4 %copy-start.2 = (bf16[512,1024]{1,0:T(8,128)(2,1)S(1)}, bf16[512,1024]{1,0:T(8,128)(2,1)}, u32[]{:S(2)}) copy-start(bf16[512,1024]{1,0:T(8,128)(2,1)} %param.8) | copy-start | bytes 3145732
  13.7 121.7 %copy-start.3 = (s32[512]{0:T(512)S(1)}, s32[512]{0:T(512)}, u32[]{:S(2)}) copy-start(s32[512]{0:T(512)} %param.10) | copy-start | bytes 6148
  218.9 1.0 copy-start.1
Sparse Core Ops, SparseCore 0:
  11.2 99.7 all-gather.1
  219.0 244.2 reduce-scatter.1
where the time goes:
time: 477 us; the launch traced here: 475 us
  waiting for transfers between devices  340 us (71%)
  blocking collectives  83.3 us (17%)
  matrix products  20.7 us (4%)
  between operations  16.7 us (4%)
  other arithmetic  8.77 us (2%)
  local copies, waits for them, and re-layouts  5.11 us (1%)
    reduce_scatter x1, waiting for transfers between devices, shards(): lax.psum_scatter(lax.dot_general(noise_left, scaled, dims, preferred_elem...  243 us
    all_gather x1, waiting for transfers between devices, shards(): lax.all_gather(weight_half, 'pop', axis=0, tiled=True)  97.2 us
    psum x1, blocking collectives, shards(): lax.psum((jnp.sum(raw_fitness), jnp.sum(raw_fitness * raw_fitness)), 'pop')  69.2 us
    psum x1, blocking collectives, shards(): reward = lax.psum(partial_value, 'wa')  14.1 us
    dot_general x1, matrix products, shards(): lax.dot_general(noise_left, scaled, dims, preferred_element_type=jnp.floa...  10.4 us
  transfers between devices with their start and end apart: 2, of which 2 were waited for; matrix products, arithmetic and copies ran while one was open for 1% of the time, Pallas kernels for 0%

commit v1 on v0

v1 whole, which is shorter than its diff:
```python
import math

import jax
import jax.numpy as jnp
from jax import lax
from jax.experimental import pallas as pl
from jax.experimental.pallas import tpu as pltpu
from jax.sharding import PartitionSpec as P

D = 4096
F = 8192
NZ, NY, NX = 8, 4, 4
MEMBERS = 512
POPULATION = MEMBERS * NZ * NY
OTHERS = 3 * MEMBERS // 2
SHARE = 64

noise_scale = 0.5
learn_rate = 0.01
epsilon = 1e-05

bf16 = jnp.bfloat16
f32 = jnp.float32


def move(value, dz, dy):
    pairs = [
        (z * NY + y, (z + dz) % NZ * NY + (y + dy) % NY)
        for z in range(NZ)
        for y in range(NY)
    ]
    return lax.ppermute(value, "pop", pairs)


def swap_pop(value, mask):
    return lax.ppermute(value, "pop", [(i, i ^ mask) for i in range(NZ * NY)])


def swap_wa(value, mask):
    return lax.ppermute(value, "wa", [(i, i ^ mask) for i in range(2 * NX)])


def move_x(value, dx):
    pairs = [
        (2 * x + c, 2 * ((x + dx) % NX) + c) for x in range(NX) for c in range(2)
    ]
    return lax.ppermute(value, "wa", pairs)


def forward_kernel(pieces, has_total, last, place, inputs, line, other_line, *refs):
    refs = list(refs)
    pieces_in = [refs.pop(0) for _ in pieces]
    total_in = refs.pop(0) if has_total else None
    if last:
        projected, right, right_partner, probe = [refs.pop(0) for _ in range(4)]
    out = refs.pop(0)
    total = refs.pop(0) if last else out
    weights, gathered, arrived = refs
    z, x, core = place[0], place[1], place[2]
    copies, at = [], 0
    for index, ((dz, first, depth), piece) in enumerate(zip(pieces, pieces_in)):
        here = pl.ds(at, depth)
        columns = pl.ds(pl.multiple_of(lax.rem(z + dz, NZ) * 512 + first, 128), depth)
        moves = [
            (piece, weights.at[here, :]),
            (inputs.at[:, columns], gathered.at[pl.ds(0, MEMBERS), here]),
        ]
        for dx in range(NX):
            owner = 2 * lax.rem(x + dx, NX)
            for source, rest in ((line, core), (other_line, 1 - core)):
                row = pl.multiple_of(MEMBERS + (owner + rest) * SHARE, SHARE)
                moves.append(
                    (
                        source.at[pl.ds(dx * SHARE, SHARE), columns],
                        gathered.at[pl.ds(row, SHARE), here],
                    )
                )
        for number, (source, target) in enumerate(moves):
            copies.append(
                pltpu.make_async_copy(source, target, arrived.at[index * len(moves) + number])
            )
            copies[-1].start()
        at += depth
    at, each = 0, len(copies) // len(pieces)
    for index, (_, _, depth) in enumerate(pieces):
        for copy in copies[index * each : (index + 1) * each]:
            copy.wait()
        for row in range(0, 2 * MEMBERS, 256):
            rows = pl.ds(row, 256)
            term = jnp.dot(
                gathered[rows, at : at + depth],
                weights[at : at + depth, :],
                preferred_element_type=f32,
            )
            if index:
                term = term + total[rows, :]
            elif has_total:
                term = term + total_in[rows, :]
            total[rows, :] = term
        at += depth
    if last:
        for group in range(2 * MEMBERS // 128):
            own = group < MEMBERS // 128
            rows = pl.ds(group * 128, 128)
            noise = right if own else right_partner
            noise_rows = pl.ds(group % (MEMBERS // 128) * 128, 128)
            wide = noise_scale * jnp.transpose(
                jnp.broadcast_to(projected[group : group + 1, :], (128, 128))
            )
            terms = jnp.zeros((128, 128), f32)
            for lane in range(0, 512, 128):
                lanes = pl.ds(lane, 128)
                outputs = total[rows, lanes] + wide * noise[noise_rows, lanes].astype(f32)
                terms = terms + jnp.tanh(outputs) * probe[:, lanes]
            out[pl.ds(group, 1), :] = jnp.sum(
                jnp.transpose(terms), axis=0, keepdims=True
            ) / math.sqrt(F)


def forward(place, rows, pieces, total=None, tail=None):
    plan = tuple(piece[:3] for piece in pieces)
    depth = sum(piece[2] for piece in pieces)
    vmem, hbm = pl.BlockSpec(memory_space=pltpu.VMEM), pl.BlockSpec(memory_space=pl.ANY)
    near = ([] if total is None else [total]) + ([] if tail is None else tail)
    scratch = [] if tail is None else [pltpu.VMEM((2 * MEMBERS, 512), f32)]
    scratch += [
        pltpu.VMEM((depth, 512), bf16),
        pltpu.VMEM((2 * MEMBERS, depth), bf16),
        pltpu.SemaphoreType.DMA((len(pieces) * (2 + 2 * NX),)),
    ]
    return pl.pallas_call(
        lambda *refs: forward_kernel(plan, total is not None, tail is not None, *refs),
        in_specs=[pl.BlockSpec(memory_space=pltpu.SMEM)]
        + [hbm] * (3 + len(pieces))
        + [vmem] * len(near),
        out_specs=vmem,
        out_shape=jax.ShapeDtypeStruct((2 * MEMBERS, 512) if tail is None else (8, 128), f32),
        scratch_shapes=scratch,
        compiler_params=pltpu.CompilerParams(vmem_limit_bytes=60 * 2**20),
        cost_estimate=pl.CostEstimate(
            flops=2 * 2 * MEMBERS * depth * 512,
            bytes_accessed=depth * 2 * 1536 + 4 * 2**20,
            transcendentals=0,
        ),
    )(place, *rows, *[piece[3] for piece in pieces], *near)


def update_kernel(place, left, line, other_line, right, right_line, right_other, out):
    total = update_dot(left[...], right[...])
    total += update_dot(line[...], right_line[...])
    out[0] = total + update_dot(other_line[...], right_other[...])


def first_kernel(
    place, sums, left, line, other_line, raw, right, right_1, right_2, right_3, *outs
):
    up, down, fitness, scaled, scaled_line, scaled_other = outs
    x, core = place[1], place[2]

    def total_of(tile):
        return jnp.sum(jnp.sum(tile, axis=1, keepdims=True), axis=0, keepdims=True)

    center = total_of(sums[:4, :]) / POPULATION
    spread = total_of(sums[4:, :]) / POPULATION - center * center
    scale = lax.rsqrt(spread + epsilon)
    fitness[...] = (raw[:4, :] - center) * scale

    def wide(row):
        fit = (raw[row, :] - center) * scale / math.sqrt(POPULATION)
        return jnp.transpose(jnp.broadcast_to(fit, (128, 128)))

    def store(target, at, count, fit, values):
        for lane in range(0, 512, 128):
            lanes = pl.ds(lane, 128)
            target[pl.ds(at, count), lanes] = (
                fit * values[:, lane : lane + 128].astype(f32)
            ).astype(bf16)

    for row in range(4):
        store(scaled, row * 128, 128, wide(pl.ds(row, 1)), right[pl.ds(row * 128, 128), :])
    at = 0
    for dx in range(NX):
        owner = lax.rem(x + dx, NX)
        for index, values in enumerate((right_1, right_2, right_3)):
            fit = wide(pl.ds(4 * index + 4 + owner, 1))
            low, high = fit[:SHARE], fit[SHARE:]
            for target, side in ((scaled_line, core), (scaled_other, 1 - core)):
                row = pl.multiple_of((2 * owner + side) * SHARE, SHARE)
                store(
                    target,
                    at,
                    SHARE,
                    jnp.where(side == 0, low, high),
                    values[pl.ds(row, SHARE), :],
                )
            at += SHARE
    total = update_dot(left[...], scaled[...])
    total += update_dot(line[...], scaled_line[...])
    total += update_dot(other_line[...], scaled_other[...])
    up[...] = total[:, :256].astype(bf16)
    down[...] = total[:, 256:].astype(bf16)


def left_specs(distance):
    return [
        pl.BlockSpec(
            (MEMBERS, 256),
            lambda i, s: (0, lax.rem(s[0] + distance(i), NZ) * 2 + s[3]),
        )
    ] + [
        pl.BlockSpec((OTHERS, 256), lambda i, s: (0, lax.rem(s[0] + distance(i), NZ)))
    ] * 2


def whole(shape, space=pltpu.VMEM):
    return pl.BlockSpec(shape, lambda i, s: (0,) * len(shape), memory_space=space)


def update_first(place, sums, left, line, other_line, raw, rights):
    shapes = [(MEMBERS, 512), (OTHERS, 512), (OTHERS, 512)]
    return pl.pallas_call(
        first_kernel,
        grid_spec=pltpu.PrefetchScalarGridSpec(
            num_scalar_prefetch=1,
            grid=(1,),
            in_specs=[whole((8, 128))]
            + left_specs(lambda i: 4)
            + [whole((16, 128))]
            + [whole((MEMBERS, 512))] * 4,
            out_specs=[whole((256, 256))] * 2
            + [whole((4, 128))]
            + [whole(shape) for shape in shapes],
        ),
        out_shape=[jax.ShapeDtypeStruct((256, 256), bf16)] * 2
        + [jax.ShapeDtypeStruct((4, 128), f32)]
        + [jax.ShapeDtypeStruct(shape, bf16) for shape in shapes],
        compiler_params=pltpu.CompilerParams(vmem_limit_bytes=40 * 2**20),
        cost_estimate=pl.CostEstimate(
            flops=2 * 2048 * 256 * 512, bytes_accessed=6 * 2**20, transcendentals=0
        ),
    )(place, sums, left, line, other_line, raw, *rights)


def update_rest(place, left, line, other_line, right, right_line, right_other, count, distance):
    return pl.pallas_call(
        update_kernel,
        grid_spec=pltpu.PrefetchScalarGridSpec(
            num_scalar_prefetch=1,
            grid=(count,),
            in_specs=left_specs(distance)
            + [whole((MEMBERS, 512)), whole((OTHERS, 512)), whole((OTHERS, 512))],
            out_specs=pl.BlockSpec((1, 256, 512), lambda i, s: (i, 0, 0)),
        ),
        out_shape=jax.ShapeDtypeStruct((count, 256, 512), f32),
        compiler_params=pltpu.CompilerParams(vmem_limit_bytes=40 * 2**20),
        cost_estimate=pl.CostEstimate(
            flops=2 * 2048 * 256 * 512, bytes_accessed=2**20, transcendentals=0
        ),
    )(place, left, line, other_line, right, right_line, right_other)


def update_dot(left, right):
    return lax.dot_general(
        left, right, (((0,), (0,)), ((), ())), preferred_element_type=f32
    )


def after(value, *others):
    return lax.optimization_barrier((value, *others))[0]


def shards(inputs, noise_left, noise_right, reward_probe, scores, master):
    pop, wa = lax.axis_index("pop"), lax.axis_index("wa")
    z, y = pop // NY, pop % NY
    x, core = wa // 2, wa % 2
    half, parity = y // 2, y % 2
    place = jnp.stack([z, x, core, half]).astype(jnp.int32)

    def halves(value):
        return (
            lax.dynamic_slice_in_dim(value, parity * 512, 512, 1),
            lax.dynamic_slice_in_dim(value, (1 - parity) * 512, 512, 1),
        )

    weight_own, weight_not = halves(master.astype(bf16))
    rel = [
        weight_own,
        swap_pop(weight_not, 1),
        swap_pop(weight_own, 2),
        swap_pop(weight_not, 3),
    ]
    odd, high = parity == 1, half == 1
    rel = [jnp.where(odd, rel[i ^ 1], rel[i]) for i in range(NY)]
    whole_y = jnp.concatenate([jnp.where(high, rel[i ^ 2], rel[i]) for i in range(NY)])

    share = lax.dynamic_slice_in_dim(inputs, wa * SHARE, SHARE, 0)
    share = swap_pop(share, 1)
    up1, down1 = move(whole_y, -1, 0), move(whole_y, 1, 0)
    share = after(share, whole_y)
    inputs_line = jnp.concatenate(
        [share, move_x(share, -1), move_x(share, 2), move_x(share, 1)]
    )

    projected = jnp.sum(inputs.astype(f32) * noise_left.astype(f32), axis=1) / math.sqrt(D)
    projected = projected.reshape(4, 128)
    share = lax.dynamic_slice_in_dim(noise_left, wa * SHARE, SHARE, 0)
    share = jnp.swapaxes(share.reshape(SHARE, NZ, 2, 256), 0, 2).swapaxes(1, 2)
    share = share.reshape(2, SHARE, D // 2)
    share_own = lax.dynamic_index_in_dim(share, half, 0, keepdims=False)
    share_not = lax.dynamic_index_in_dim(share, 1 - half, 0, keepdims=False)
    right_own, right_not = halves(noise_right)

    up2, down2 = move(up1, -1, 0), move(down1, 1, 0)
    inputs_other = swap_wa(after(inputs_line, up1, down1), 1)
    left_1 = swap_pop(after(share_own, up1, down1, inputs_line), 1)
    left_2 = swap_pop(after(share_not, up1, down1, inputs_line), 2)
    rows = (inputs, inputs_line, inputs_other)

    up3, down3 = move(up2, -1, 0), move(down2, 1, 0)
    left_3 = swap_pop(after(share_not, up2, down2, left_1, left_2), 3)
    right_1 = swap_pop(after(right_not, up2, down2, left_1), 1)
    right_3 = swap_pop(after(right_not, up2, down2, left_2), 3)
    total = forward(
        place, rows, [(0, 0, 512, whole_y), (1, 0, 512, up1), (7, 0, 512, down1)]
    )

    up4, down4 = move(up3[:256], -1, 0), move(down3[256:], 1, 0)
    fetched = after(jnp.concatenate([left_1, left_2, left_3]), up3, down3, right_1, total)
    line_1, line_3 = move_x(fetched, -1), move_x(fetched, 1)
    projected = jnp.concatenate([projected, swap_pop(after(projected, right_1), 1)])
    right_2 = swap_pop(after(right_own, up3, down3, right_3), 2)
    total = forward(
        place,
        rows,
        [(2, 0, 512, up2), (6, 0, 512, down2), (3, 0, 512, up3), (5, 0, 512, down3)],
        total,
    )
    probe = lax.dynamic_slice_in_dim(reward_probe, parity * 512, 512, 0).reshape(1, 512)
    reward = forward(
        place,
        rows,
        [(4, 0, 256, up4), (4, 256, 256, down4)],
        total,
        [projected, right_own, right_1, probe],
    )
    line_2 = move_x(after(fetched, line_1, line_3, total), 2)
    line = jnp.concatenate([fetched, line_1, line_2, line_3])
    other_line = swap_wa(line, 1)

    for mask in (1, 2, 4):
        reward = reward + swap_wa(reward, mask)
    own = reward[:4] + scores.astype(f32).reshape(4, 128) / 16.0
    reward = jnp.concatenate([own, reward[4:]])
    others = [swap_pop(reward, mask) for mask in (1, 2, 3)]
    raw = [
        own + others[0][4:],
        reward[4:] + others[0][:4],
        others[1][:4] + others[2][4:],
        others[1][4:] + others[2][:4],
    ]
    sums = jnp.concatenate(
        [raw[0] + raw[1] + raw[2] + raw[3], sum(tile * tile for tile in raw)]
    )
    for mask in (NY, 2 * NY, 4 * NY):
        sums = sums + swap_pop(sums, mask)

    up, down, fitness, *scaled = update_first(
        place,
        sums,
        noise_left,
        line,
        other_line,
        jnp.concatenate(raw),
        (right_own, right_1, right_2, right_3),
    )
    members = (place, noise_left, line, other_line, *scaled)
    next_parts = update_rest(*members, 2, lambda i: 3 + 2 * i)
    up = move(up, 1, 0).astype(f32)
    down = move(down, -1, 0).astype(f32)
    none = jnp.zeros((256, 256), f32)
    up = jnp.concatenate([up, none], axis=1)
    down = jnp.concatenate([none, down], axis=1)
    parts = update_rest(
        *members,
        5,
        lambda i: jnp.where(i == 4, 0, jnp.where(lax.rem(i, 2) == 0, 2 - i // 2, 6 + i // 2)),
    )
    for up_part, down_part in (
        (next_parts[0], next_parts[1]),
        (parts[0], parts[1]),
        (parts[2], parts[3]),
    ):
        up = move((up_part + up).astype(bf16), 1, 0).astype(f32)
        down = move((down_part + down).astype(bf16), -1, 0).astype(f32)
    rows = (parts[4] + up + down).reshape(2, 128, 512)
    mine = lax.dynamic_index_in_dim(rows, parity, 0, keepdims=False)
    theirs = lax.dynamic_index_in_dim(rows, 1 - parity, 0, keepdims=False)
    received = swap_pop(theirs.astype(bf16), 1).astype(f32)
    update = jnp.where(
        parity == 0,
        jnp.concatenate([mine, received], axis=1),
        jnp.concatenate([received, mine], axis=1),
    )
    new_master = master + learn_rate * update
    return (fitness.reshape(MEMBERS), update, new_master, new_master.astype(bf16))


def solution(mesh):
    return jax.shard_map(
        shards,
        mesh=mesh,
        in_specs=(
            P("pop", None),
            P("pop", None),
            P("pop", "wa"),
            P("wa"),
            P("pop"),
            P("pop", "wa"),
        ),
        out_specs=(P("pop"), P("pop", "wa"), P("pop", "wa"), P("pop", "wa")),
        check_vma=False,
    )
```

time: 477 us -> 260 us (0.55)
  waiting for transfers between devices: 340 us -> 129 us
  blocking collectives: 83.3 us -> 0 us
  starting transfers between devices: 0.08 us -> 69.8 us
  Pallas kernels: 0 us -> 30.9 us
  matrix products: 20.7 us -> 0 us
  between operations: 16.7 us -> 1.35 us
  local copies, waits for them, and re-layouts: 5.11 us -> 14 us
    reduce_scatter x1 -> x0, waiting for transfers between devices: 243 us -> none  [shards(): lax.psum_scatter(lax.dot_general(noise_left, scaled, dims, preferred_elem...]
    ppermute x0 -> x45, waiting for transfers between devices: none -> 129 us  [the longest x6 47.6 us: move_x(): return lax.ppermute(value, 'wa', pairs)]
    all_gather x1 -> x0, waiting for transfers between devices: 97.2 us -> none  [shards(): lax.all_gather(weight_half, 'pop', axis=0, tiled=True)]
    psum x2 -> x0, blocking collectives: 83.3 us -> none  [the longest x1 69.2 us: shards(): lax.psum((jnp.sum(raw_fitness), jnp.sum(raw_fitness * raw_fitness)), 'pop')]
    ppermute x0 -> x45, starting transfers between devices: none -> 69.8 us  [the longest x16 25.8 us: move(): return lax.ppermute(value, 'pop', pairs)]
    pallas_call x0 -> x6, Pallas kernels: none -> 30.9 us  [the longest x3 17.8 us: forward(): pl.pallas_call(lambda *refs: forward_kernel(plan, total is not None, tail...]
    dot_general x3 -> x0, matrix products: 20.7 us -> none  [the longest x1 10.4 us: shards(): lax.dot_general(noise_left, scaled, dims, preferred_element_type=jnp.floa...]
    dynamic_slice x0 -> x5, local copies, waits for them, and re-layouts: none -> 5.1 us  [the longest x1 2.26 us: halves(): lax.dynamic_slice_in_dim(value, parity * 512, 512, 1)]
  transfers between devices with their start and end apart: 2 -> 45, of which waited for: 2 -> 31; matrix products, arithmetic and copies ran while one was open for 1% -> 7% of each run, Pallas kernels for 0% -> 11%
where the time goes in v1:
time: 260 us; the launch traced here: 256 us
  waiting for transfers between devices  129 us (50%)
  starting transfers between devices  69.8 us (27%)
  Pallas kernels  30.9 us (12%)
  local copies, waits for them, and re-layouts  14 us (5%)
  other arithmetic  10.5 us (4%)
    ppermute x6, waiting for transfers between devices, move_x(): return lax.ppermute(value, 'wa', pairs)  47.6 us
    ppermute x16, waiting for transfers between devices, move(): return lax.ppermute(value, 'pop', pairs)  37.7 us
    ppermute x18, waiting for transfers between devices, swap_pop(): return lax.ppermute(value, 'pop', [(i, i ^ mask) for i in range(NZ * NY)])  35.1 us
    ppermute x16, starting transfers between devices, move(): return lax.ppermute(value, 'pop', pairs)  25.8 us
    ppermute x18, starting transfers between devices, swap_pop(): return lax.ppermute(value, 'pop', [(i, i ^ mask) for i in range(NZ * NY)])  25.1 us
    pallas_call x3, Pallas kernels, forward(): pl.pallas_call(lambda *refs: forward_kernel(plan, total is not None, tail...  17.8 us
    ppermute x5, starting transfers between devices, swap_wa(): return lax.ppermute(value, 'wa', [(i, i ^ mask) for i in range(2 * NX)])  11.7 us
    pallas_call x2, Pallas kernels, update_rest(): pl.pallas_call(update_kernel, grid_spec=pltpu.PrefetchScalarGridSpec(num_...  9.36 us
  transfers between devices with their start and end apart: 45, of which 31 were waited for; matrix products, arithmetic and copies ran while one was open for 7% of the time, Pallas kernels for 11%

profile of v1, /device:TPU:16, one launch (start us, length us, event | category | flops | bytes accessed | tf_op | source)
XLA Modules:
  0.0 256.0 jit_solution(2639578043128986953)
XLA Ops:
  0.6 1.1 constant_dynamic-slice_fusion.5
  1.7 1.4 collective-permute-start
  3.1 1.1 convert_element_type.62
  4.2 1.4 collective-permute-start.1
  5.7 1.5 collective-permute-start.2
  7.1 1.3 collective-permute-start.3
  9.3 10.2 %collective-permute-done.2 = bf16[128,512]{1,0:T(8,128)(2,1)S(1)} collective-permute-done((bf16[128,512]{1,0:T(8,128)(2,1)S(1)}, bf16[128,512]{1,0:T(8,128)(2,1)S(1)}, u32[]{:S(2)}, u32[]{:S(2)}) %collective-permute-start.2) | collective-permute-done | bytes 131104 | tf_op jit(solution)/shard_map/ppermute | solution.py:36
  19.5 1.6 collective-permute-done.3
  21.2 2.8 %collective-permute-start.4 = (bf16[64,4096]{1,0:T(8,128)(2,1)S(1)}, bf16[64,4096]{1,0:T(8,128)(2,1)S(1)}, u32[]{:S(2)}, u32[]{:S(2)}) collective-permute-start(bf16[64,4096]{1,0:T(8,128)(2,1)S(1)} %collective-permute-done), channel_id=1, source_target_pairs={{0,6},{1,7},{2,0},{3,1},{4,2},{5,3},{6,4},{7,5},{8,14},{9,15},{10,... | collective-permute-start | bytes 1572872 | tf_op jit(solution)/shard_map/ppermute | solution.py:47
  24.0 5.9 %collective-permute-start.7 = (bf16[512,512]{1,0:T(8,128)(2,1)S(1)}, bf16[512,512]{1,0:T(8,128)(2,1)}, u32[]{:S(2)}, u32[]{:S(2)}) collective-permute-start(bf16[512,512]{1,0:T(8,128)(2,1)S(1)} %pad_maximum_fusion.1.refs_4_), channel_id=1, source_target_pairs={{0,224},{8,232},{16,240},{24,248},{32,0},{40,8},{48,16},{56,24},{6... | collective-permute-start | bytes 1572872 | tf_op jit(solution)/shard_map/ppermute | solution.py:32
  31.7 13.9 %collective-permute-done.4 = bf16[64,4096]{1,0:T(8,128)(2,1)S(1)} collective-permute-done((bf16[64,4096]{1,0:T(8,128)(2,1)S(1)}, bf16[64,4096]{1,0:T(8,128)(2,1)S(1)}, u32[]{:S(2)}, u32[]{:S(2)}) %collective-permute-start.4) | collective-permute-done | bytes 524320 | tf_op jit(solution)/shard_map/ppermute | solution.py:47
  46.3 8.6 %collective-permute-done.6 = bf16[64,4096]{1,0:T(8,128)(2,1)S(1)} collective-permute-done((bf16[64,4096]{1,0:T(8,128)(2,1)S(1)}, bf16[64,4096]{1,0:T(8,128)(2,1)S(1)}, u32[]{:S(2)}, u32[]{:S(2)}) %collective-permute-start.6) | collective-permute-done | bytes 524320 | tf_op jit(solution)/shard_map/ppermute | solution.py:47
  55.1 3.0 %collective-permute-start.10 = (bf16[512,512]{1,0:T(8,128)(2,1)}, bf16[512,512]{1,0:T(8,128)(2,1)}, u32[]{:S(2)}, u32[]{:S(2)}) collective-permute-start(bf16[512,512]{1,0:T(8,128)(2,1)} %collective-permute-done.7.refs_5_), channel_id=1, source_target_pairs={{0,224},{8,232},{16,240},{24,248},{32,0},{40,8},{48,16},{56,24},{6... | collective-permute-start | bytes 1572872 | tf_op jit(solution)/shard_map/ppermute | solution.py:32
  58.1 1.1 constant_dynamic-slice_fusion.1
  60.4 1.3 reshape.32
  61.8 1.4 collective-permute-start.16
  63.8 6.4 %collective-permute-done.10.refs_4_ = bf16[512,512]{1,0:T(8,128)(2,1)} collective-permute-done((bf16[512,512]{1,0:T(8,128)(2,1)}, bf16[512,512]{1,0:T(8,128)(2,1)}, u32[]{:S(2)}, u32[]{:S(2)}) %collective-permute-start.10) | collective-permute-done | bytes 524320 | tf_op jit(solution)/shard_map/ppermute | solution.py:32
  70.2 3.4 %collective-permute-done.13.refs_5_ = bf16[512,512]{1,0:T(8,128)(2,1)} collective-permute-done((bf16[512,512]{1,0:T(8,128)(2,1)}, bf16[512,512]{1,0:T(8,128)(2,1)}, u32[]{:S(2)}, u32[]{:S(2)}) %collective-permute-start.13) | collective-permute-done | bytes 524320 | tf_op jit(solution)/shard_map/ppermute | solution.py:32
  73.6 2.1 collective-permute-done.28
  75.7 1.6 collective-permute-start.29
  77.3 2.3 constant_dynamic-slice_fusion
  79.6 3.0 %collective-permute-start.11 = (bf16[512,512]{1,0:T(8,128)(2,1)}, bf16[512,512]{1,0:T(8,128)(2,1)}, u32[]{:S(2)}, u32[]{:S(2)}) collective-permute-start(bf16[512,512]{1,0:T(8,128)(2,1)} %collective-permute-done.10.refs_4_), channel_id=1, source_target_pairs={{0,224},{8,232},{16,240},{24,248},{32,0},{40,8},{48,16},{56,24},{6... | collective-permute-start | bytes 1572872 | tf_op jit(solution)/shard_map/ppermute | solution.py:32
  82.8 2.6 %collective-permute-start.17 = (bf16[512,512]{1,0:T(8,128)(2,1)}, bf16[512,512]{1,0:T(8,128)(2,1)S(1)}, u32[]{:S(2)}, u32[]{:S(2)}) collective-permute-start(bf16[512,512]{1,0:T(8,128)(2,1)} %get-tuple-element.30), channel_id=1, source_target_pairs={{0,8},{8,0},{16,24},{24,16},{32,40},{40,32},{48,56},{56,48},{64,72... | collective-permute-start | bytes 1572872 | tf_op jit(solution)/shard_map/ppermute | solution.py:36
  86.0 1.2 pad_maximum_fusion
  87.1 5.6 %shard_map.93.refs_8_ = f32[1024,512]{1,0:T(8,128)} custom-call(s32[4]{0:T(128)} %pad_add_fusion.refs_0_.place, bf16[512,4096]{1,0:T(8,128)(2,1)} %refs_1_.5, bf16[256,4096]{1,0:T(8,128)(2,1)} %copy-done.7, bf16[256,4096]{1,0:T(8,128)(2,1)} %collective-permute-done.9.refs_3_, bf16[512,512]{1,0:T(8,128)(2,1)} %copy-done.9, ...), custom_call_target="tpu_custom_call" | custom-call | flops 1610612736 | bytes 8912896 | tf_op jit(solution)/shard_map/pallas_call | solution.py:131
  92.9 3.6 %collective-permute-done.14.refs_7_ = bf16[512,512]{1,0:T(8,128)(2,1)} collective-permute-done((bf16[512,512]{1,0:T(8,128)(2,1)}, bf16[512,512]{1,0:T(8,128)(2,1)}, u32[]{:S(2)}, u32[]{:S(2)}) %collective-permute-start.14) | collective-permute-done | bytes 524320 | tf_op jit(solution)/shard_map/ppermute | solution.py:32
  97.2 1.4 collective-permute-start.31
  98.6 7.3 %shard_map.94.refs_6_ = f32[1024,512]{1,0:T(8,128)} custom-call(s32[4]{0:T(128)} %pad_add_fusion.refs_0_.place, bf16[512,4096]{1,0:T(8,128)(2,1)} %refs_1_.5, bf16[256,4096]{1,0:T(8,128)(2,1)} %copy-done.7, bf16[256,4096]{1,0:T(8,128)(2,1)} %collective-permute-done.9.refs_3_, bf16[512,512]{1,0:T(8,128)(2,1)} %collective-permute-done.10.refs_4_, ...), custom_call_target="tpu_custom_call" | custom-call | flops 2147483648 | bytes 10485760 | tf_op jit(solution)/shard_map/pallas_call | solution.py:131
  105.9 7.7 %collective-permute-done.30 = bf16[192,2048]{1,0:T(8,128)(2,1)S(1)} collective-permute-done((bf16[192,2048]{1,0:T(8,128)(2,1)S(1)}, bf16[192,2048]{1,0:T(8,128)(2,1)S(1)}, u32[]{:S(2)}, u32[]{:S(2)}) %collective-permute-start.30) | collective-permute-done | bytes 786464 | tf_op jit(solution)/shard_map/ppermute | solution.py:47
  113.6 1.5 collective-permute-done.31
  116.6 1.4 constant_dynamic-update-slice_fusion.6
  117.9 15.3 %collective-permute-done.32 = bf16[192,2048]{1,0:T(8,128)(2,1)S(1)} collective-permute-done((bf16[192,2048]{1,0:T(8,128)(2,1)S(1)}, bf16[192,2048]{1,0:T(8,128)(2,1)S(1)}, u32[]{:S(2)}, u32[]{:S(2)}) %collective-permute-start.32) | collective-permute-done | bytes 786464 | tf_op jit(solution)/shard_map/ppermute | solution.py:47
  133.5 3.5 %multiply_reduce_fusion = f32[512]{0:T(512)S(1)} fusion(bf16[512,4096]{1,0:T(8,128)(2,1)S(1)} %copy-done, bf16[512,4096]{1,0:T(8,128)(2,1)} %refs_1_.5), kind=kLoop, calls=%fused_computation | loop fusion | flops 8388096 | bytes 8390656 | tf_op jit(solution)/shard_map/reduce_sum | solution.py:304
  138.5 2.2 collective-permute-start.12
  141.8 2.6 %collective-permute-start.18 = (f32[4,128]{1,0:T(4,128)S(1)}, f32[4,128]{1,0:T(4,128)S(1)}, u32[]{:S(2)}, u32[]{:S(2)}) collective-permute-start(f32[4,128]{1,0:T(4,128)S(1)} %multiply_bitcast_fusion), channel_id=1, source_target_pairs={{0,8},{8,0},{16,24},{24,16},{32,40},{40,32},{48,56},{56,48},{64,72... | collective-permute-start | bytes 6152 | tf_op jit(solution)/shard_map/ppermute | solution.py:36
  147.0 4.4 %collective-permute-done.15.refs_5_ = bf16[256,512]{1,0:T(8,128)(2,1)S(1)} collective-permute-done((bf16[256,512]{1,0:T(8,128)(2,1)S(1)}, bf16[256,512]{1,0:T(8,128)(2,1)S(1)}, u32[]{:S(2)}, u32[]{:S(2)}) %collective-permute-start.15) | collective-permute-done | bytes 262176 | tf_op jit(solution)/shard_map/ppermute | solution.py:32
  152.2 4.9 %shard_map.95 = f32[8,128]{1,0:T(8,128)} custom-call(s32[4]{0:T(128)} %pad_add_fusion.refs_0_.place, bf16[512,4096]{1,0:T(8,128)(2,1)} %refs_1_.5, bf16[256,4096]{1,0:T(8,128)(2,1)} %copy-done.7, bf16[256,4096]{1,0:T(8,128)(2,1)} %collective-permute-done.9.refs_3_, bf16[256,512]{1,0:T(8,128)(2,1)} %copy-done.13, bf16[256,512]{1,0:T(8,128)(2,1)} %copy-done.14, ...), custom_call_target="tpu_custom_call" | custom-call | flops 536870912 | bytes 5767168 | tf_op jit(solution)/shard_map/pallas_call | solution.py:131
  157.1 10.4 %collective-permute-start.19 = (f32[8,128]{1,0:T(8,128)}, f32[8,128]{1,0:T(8,128)S(1)}, u32[]{:S(2)}, u32[]{:S(2)}) collective-permute-start(f32[8,128]{1,0:T(8,128)} %shard_map.95), channel_id=1, source_target_pairs={{0,1},{1,0},{2,3},{3,2},{4,5},{5,4},{6,7},{7,6},{8,9},{9,8},{10,11... | collective-permute-start | bytes 12296 | tf_op jit(solution)/shard_map/ppermute | solution.py:40
  167.5 1.4 collective-permute-done.19
  169.7 3.4 %collective-permute-done.20 = f32[8,128]{1,0:T(8,128)S(1)} collective-permute-done((f32[8,128]{1,0:T(8,128)S(1)}, f32[8,128]{1,0:T(8,128)S(1)}, u32[]{:S(2)}, u32[]{:S(2)}) %collective-permute-start.20) | collective-permute-done | bytes 4128 | tf_op jit(solution)/shard_map/ppermute | solution.py:40
  174.1 4.2 %collective-permute-done.21 = f32[8,128]{1,0:T(8,128)S(1)} collective-permute-done((f32[8,128]{1,0:T(8,128)S(1)}, f32[8,128]{1,0:T(8,128)S(1)}, u32[]{:S(2)}, u32[]{:S(2)}) %collective-permute-start.21) | collective-permute-done | bytes 4128 | tf_op jit(solution)/shard_map/ppermute | solution.py:40
  178.3 1.7 collective-permute-start.22
  179.9 2.0 collective-permute-start.24
  182.5 3.0 %collective-permute-start.35 = (bf16[512,512]{1,0:T(8,128)(2,1)S(1)}, bf16[512,512]{1,0:T(8,128)(2,1)S(1)}, u32[]{:S(2)}, u32[]{:S(2)}) collective-permute-start(bf16[512,512]{1,0:T(8,128)(2,1)S(1)} %copy-done.3), channel_id=1, source_target_pairs={{0,16},{8,24},{16,0},{24,8},{32,48},{40,56},{48,32},{56,40},{64,80... | collective-permute-start | bytes 1572872 | tf_op jit(solution)/shard_map/ppermute | solution.py:36
  185.4 1.7 collective-permute-done.23
  187.2 3.6 %collective-permute-done.25 = f32[8,128]{1,0:T(8,128)S(1)} collective-permute-done((f32[8,128]{1,0:T(8,128)S(1)}, f32[8,128]{1,0:T(8,128)S(1)}, u32[]{:S(2)}, u32[]{:S(2)}) %collective-permute-start.25) | collective-permute-done | bytes 4128 | tf_op jit(solution)/shard_map/ppermute | solution.py:36
  191.0 4.5 %collective-permute-done.26 = f32[8,128]{1,0:T(8,128)S(1)} collective-permute-done((f32[8,128]{1,0:T(8,128)S(1)}, f32[8,128]{1,0:T(8,128)S(1)}, u32[]{:S(2)}, u32[]{:S(2)}) %collective-permute-start.26) | collective-permute-done | bytes 4128 | tf_op jit(solution)/shard_map/ppermute | solution.py:36
  195.5 1.7 collective-permute-start.27
  197.1 6.0 %collective-permute-done.27 = f32[8,128]{1,0:T(8,128)S(1)} collective-permute-done((f32[8,128]{1,0:T(8,128)S(1)}, f32[8,128]{1,0:T(8,128)S(1)}, u32[]{:S(2)}, u32[]{:S(2)}) %collective-permute-start.27) | collective-permute-done | bytes 4128 | tf_op jit(solution)/shard_map/ppermute | solution.py:36
  204.1 3.8 %shard_map.96 = (bf16[256,256]{1,0:T(8,128)(2,1)S(1)}, bf16[256,256]{1,0:T(8,128)(2,1)S(1)}, f32[4,128]{1,0:T(4,128)}, bf16[512,512]{1,0:T(8,128)(2,1)S(1)}, bf1...) custom-call(s32[4]{0:T(128)S(1)} %copy-done.6, f32[8,128]{1,0:T(8,128)S(1)} %add.147.sums, ...), custom_call_target="tpu_custom_call" | custom-call | flops 536870912 | bytes 6291456 | tf_op jit(solution)/shard_map/pallas_call | solution.py:221
  208.0 3.2 %collective-permute-start.40 = (bf16[256,256]{1,0:T(8,128)(2,1)S(1)}, bf16[256,256]{1,0:T(8,128)(2,1)S(1)}, u32[]{:S(2)}, u32[]{:S(2)}) collective-permute-start(bf16[256,256]{1,0:T(8,128)(2,1)S(1)} %get-tuple-element.37), channel_id=1, source_target_pairs={{0,224},{8,232},{16,240},{24,248},{32,0},{40,8},{48,16},{56,24},{6... | collective-permute-start | bytes 393224 | tf_op jit(solution)/shard_map/ppermute | solution.py:32
  211.2 3.2 %shard_map.98 = f32[2,256,512]{2,1,0:T(8,128)S(1)} custom-call(s32[4]{0:T(128)S(1)} %copy-done.6, bf16[512,4096]{1,0:T(8,128)(2,1)S(1)} %copy-done.1, bf16[768,2048]{1,0:T(8,128)(2,1)S(1)} %constant_dynamic-update-slice_fusion.4.line, bf16[768,2048]{1,0:T(8,128)(2,1)} %collective-permute-done.33.other_line, bf16[512,512]{1,0:T(8,128)(2,1)S(1)} %get-tuple-element.33.right, ...), custom_call_target="tpu_custom_call" | custom-call | flops 536870912 | bytes 1048576 | tf_op jit(solution)/shard_map/pallas_call | solution.py:245
  215.1 6.2 %shard_map.97 = f32[5,256,512]{2,1,0:T(8,128)S(1)} custom-call(s32[4]{0:T(128)S(1)} %copy-done.6, bf16[512,4096]{1,0:T(8,128)(2,1)} %left.5, bf16[768,2048]{1,0:T(8,128)(2,1)S(1)} %constant_dynamic-update-slice_fusion.4.line, bf16[768,2048]{1,0:T(8,128)(2,1)} %collective-permute-done.33.other_line, bf16[512,512]{1,0:T(8,128)(2,1)S(1)} %get-tuple-element.33.right, ...), custom_call_target="tpu_custom_call" | custom-call | flops 536870912 | bytes 1048576 | tf_op jit(solution)/shard_map/pallas_call | solution.py:245
  221.3 3.3 %collective-permute-start.41 = (bf16[256,512]{1,0:T(8,128)(2,1)S(1)}, bf16[256,512]{1,0:T(8,128)(2,1)S(1)}, u32[]{:S(2)}, u32[]{:S(2)}) collective-permute-start(bf16[256,512]{1,0:T(8,128)(2,1)S(1)} %get-tuple-element.49), channel_id=1, source_target_pairs={{0,224},{8,232},{16,240},{24,248},{32,0},{40,8},{48,16},{56,24},{6... | collective-permute-start | bytes 786440 | tf_op jit(solution)/shard_map/ppermute | solution.py:32
  225.6 5.4 %collective-permute-done.41 = bf16[256,512]{1,0:T(8,128)(2,1)S(1)} collective-permute-done((bf16[256,512]{1,0:T(8,128)(2,1)S(1)}, bf16[256,512]{1,0:T(8,128)(2,1)S(1)}, u32[]{:S(2)}, u32[]{:S(2)}) %collective-permute-start.41) | collective-permute-done | bytes 262176 | tf_op jit(solution)/shard_map/ppermute | solution.py:32
  230.9 4.3 %collective-permute-done.38 = bf16[256,512]{1,0:T(8,128)(2,1)S(1)} collective-permute-done((bf16[256,512]{1,0:T(8,128)(2,1)S(1)}, bf16[256,512]{1,0:T(8,128)(2,1)S(1)}, u32[]{:S(2)}, u32[]{:S(2)}) %collective-permute-start.38) | collective-permute-done | bytes 262176 | tf_op jit(solution)/shard_map/ppermute | solution.py:32
  235.4 2.0 collective-permute-start.39
  237.5 4.3 %collective-permute-done.42 = bf16[256,512]{1,0:T(8,128)(2,1)S(1)} collective-permute-done((bf16[256,512]{1,0:T(8,128)(2,1)S(1)}, bf16[256,512]{1,0:T(8,128)(2,1)S(1)}, u32[]{:S(2)}, u32[]{:S(2)}) %collective-permute-start.42) | collective-permute-done | bytes 262176 | tf_op jit(solution)/shard_map/ppermute | solution.py:32
  241.9 2.6 %collective-permute-start.43 = (bf16[256,512]{1,0:T(8,128)(2,1)S(1)}, bf16[256,512]{1,0:T(8,128)(2,1)S(1)}, u32[]{:S(2)}, u32[]{:S(2)}) collective-permute-start(bf16[256,512]{1,0:T(8,128)(2,1)S(1)} %fusion.5), channel_id=1, source_target_pairs={{0,224},{8,232},{16,240},{24,248},{32,0},{40,8},{48,16},{56,24},{6... | collective-permute-start | bytes 786440 | tf_op jit(solution)/shard_map/ppermute | solution.py:32
  244.5 3.9 %collective-permute-done.43 = bf16[256,512]{1,0:T(8,128)(2,1)S(1)} collective-permute-done((bf16[256,512]{1,0:T(8,128)(2,1)S(1)}, bf16[256,512]{1,0:T(8,128)(2,1)S(1)}, u32[]{:S(2)}, u32[]{:S(2)}) %collective-permute-start.43) | collective-permute-done | bytes 262176 | tf_op jit(solution)/shard_map/ppermute | solution.py:32
  248.4 1.1 fusion.13
  249.6 1.4 collective-permute-start.44
  251.0 3.7 %collective-permute-done.44 = bf16[128,512]{1,0:T(8,128)(2,1)S(1)} collective-permute-done((bf16[128,512]{1,0:T(8,128)(2,1)S(1)}, bf16[128,512]{1,0:T(8,128)(2,1)S(1)}, u32[]{:S(2)}, u32[]{:S(2)}) %collective-permute-start.44) | collective-permute-done | bytes 131104 | tf_op jit(solution)/shard_map/ppermute | solution.py:36
  254.7 1.2 fusion.16
  (118 shorter events, 20.5 us)
Async XLA Ops:
  1.7 19.5 %collective-permute-start = (bf16[64,4096]{1,0:T(8,128)(2,1)S(1)}, bf16[64,4096]{1,0:T(8,128)(2,1)S(1)}, u32[]{:S(2)}, u32[]{:S(2)}) collective-permute-start(bf16[64,4096]{1,0:T(8,128)(2,1)S(1)} %constant_dynamic-slice_fusion.5), channel_id=1, source_target_pairs={{0,8},{8,0},{16,24},{24,16},{32,40},{40,32},{48,56},{56,48},{64,72... | collective-permute-start | bytes 1572872 | tf_op jit(solution)/shard_map/ppermute | solution.py:36
  4.2 5.1 %collective-permute-start.1 = (bf16[128,512]{1,0:T(8,128)(2,1)S(1)}, bf16[128,512]{1,0:T(8,128)(2,1)S(1)}, u32[]{:S(2)}, u32[]{:S(2)}) collective-permute-start(bf16[128,512]{1,0:T(8,128)(2,1)S(1)} %get-tuple-element.58), channel_id=1, source_target_pairs={{0,24},{8,16},{16,8},{24,0},{32,56},{40,48},{48,40},{56,32},{64,88... | collective-permute-start | bytes 393224 | tf_op jit(solution)/shard_map/ppermute | solution.py:36
  5.7 13.9 %collective-permute-start.2 = (bf16[128,512]{1,0:T(8,128)(2,1)S(1)}, bf16[128,512]{1,0:T(8,128)(2,1)S(1)}, u32[]{:S(2)}, u32[]{:S(2)}) collective-permute-start(bf16[128,512]{1,0:T(8,128)(2,1)S(1)} %get-tuple-element.59), channel_id=1, source_target_pairs={{0,16},{8,24},{16,0},{24,8},{32,48},{40,56},{48,32},{56,40},{64,80... | collective-permute-start | bytes 393224 | tf_op jit(solution)/shard_map/ppermute | solution.py:36
  7.1 14.0 %collective-permute-start.3 = (bf16[128,512]{1,0:T(8,128)(2,1)S(1)}, bf16[128,512]{1,0:T(8,128)(2,1)S(1)}, u32[]{:S(2)}, u32[]{:S(2)}) collective-permute-start(bf16[128,512]{1,0:T(8,128)(2,1)S(1)} %get-tuple-element.58), channel_id=1, source_target_pairs={{0,8},{8,0},{16,24},{24,16},{32,40},{40,32},{48,56},{56,48},{64,72... | collective-permute-start | bytes 393224 | tf_op jit(solution)/shard_map/ppermute | solution.py:36
  21.2 33.8 %copy-start.9 = (bf16[512,512]{1,0:T(8,128)(2,1)}, bf16[512,512]{1,0:T(8,128)(2,1)S(1)}, u32[]{:S(2)}) copy-start(bf16[512,512]{1,0:T(8,128)(2,1)S(1)} %pad_maximum_fusion.1.refs_4_) | copy-start | bytes 1572868
  21.2 24.4 %collective-permute-start.4 = (bf16[64,4096]{1,0:T(8,128)(2,1)S(1)}, bf16[64,4096]{1,0:T(8,128)(2,1)S(1)}, u32[]{:S(2)}, u32[]{:S(2)}) collective-permute-start(bf16[64,4096]{1,0:T(8,128)(2,1)S(1)} %collective-permute-done), channel_id=1, source_target_pairs={{0,6},{1,7},{2,0},{3,1},{4,2},{5,3},{6,4},{7,5},{8,14},{9,15},{10,... | collective-permute-start | bytes 1572872 | tf_op jit(solution)/shard_map/ppermute | solution.py:47
  24.0 30.9 %collective-permute-start.7 = (bf16[512,512]{1,0:T(8,128)(2,1)S(1)}, bf16[512,512]{1,0:T(8,128)(2,1)}, u32[]{:S(2)}, u32[]{:S(2)}) collective-permute-start(bf16[512,512]{1,0:T(8,128)(2,1)S(1)} %pad_maximum_fusion.1.refs_4_), channel_id=1, source_target_pairs={{0,224},{8,232},{16,240},{24,248},{32,0},{40,8},{48,16},{56,24},{6... | collective-permute-start | bytes 1572872 | tf_op jit(solution)/shard_map/ppermute | solution.py:32
  29.9 25.0 %collective-permute-start.8 = (bf16[512,512]{1,0:T(8,128)(2,1)S(1)}, bf16[512,512]{1,0:T(8,128)(2,1)}, u32[]{:S(2)}, u32[]{:S(2)}) collective-permute-start(bf16[512,512]{1,0:T(8,128)(2,1)S(1)} %pad_maximum_fusion.1.refs_4_), channel_id=1, source_target_pairs={{0,32},{8,40},{16,48},{24,56},{32,64},{40,72},{48,80},{56,88},{64,... | collective-permute-start | bytes 1572872 | tf_op jit(solution)/shard_map/ppermute | solution.py:32
  29.9 16.4 %collective-permute-start.5 = (bf16[64,4096]{1,0:T(8,128)(2,1)S(1)}, bf16[64,4096]{1,0:T(8,128)(2,1)S(1)}, u32[]{:S(2)}, u32[]{:S(2)}) collective-permute-start(bf16[64,4096]{1,0:T(8,128)(2,1)S(1)} %collective-permute-done), channel_id=1, source_target_pairs={{0,4},{1,5},{2,6},{3,7},{4,0},{5,1},{6,2},{7,3},{8,12},{9,13},{10,... | collective-permute-start | bytes 1572872 | tf_op jit(solution)/shard_map/ppermute | solution.py:47
  30.7 24.1 %collective-permute-start.6 = (bf16[64,4096]{1,0:T(8,128)(2,1)S(1)}, bf16[64,4096]{1,0:T(8,128)(2,1)S(1)}, u32[]{:S(2)}, u32[]{:S(2)}) collective-permute-start(bf16[64,4096]{1,0:T(8,128)(2,1)S(1)} %collective-permute-done), channel_id=1, source_target_pairs={{0,2},{1,3},{2,4},{3,5},{4,6},{5,7},{6,0},{7,1},{8,10},{9,11},{10,... | collective-permute-start | bytes 1572872 | tf_op jit(solution)/shard_map/ppermute | solution.py:47
  54.9 6.9 %copy-start.7 = (bf16[256,4096]{1,0:T(8,128)(2,1)}, bf16[256,4096]{1,0:T(8,128)(2,1)S(1)}, u32[]{:S(2)}) copy-start(bf16[256,4096]{1,0:T(8,128)(2,1)S(1)} %constant_dynamic-update-slice_fusion.refs_2_) | copy-start | bytes 6291460
  55.0 32.2 %collective-permute-start.9 = (bf16[256,4096]{1,0:T(8,128)(2,1)S(1)}, bf16[256,4096]{1,0:T(8,128)(2,1)}, u32[]{:S(2)}, u32[]{:S(2)}) collective-permute-start(bf16[256,4096]{1,0:T(8,128)(2,1)S(1)} %constant_dynamic-update-slice_fusion.refs_2_), channel_id=1, source_target_pairs={{0,1},{1,0},{2,3},{3,2},{4,5},{5,4},{6,7},{7,6},{8,9},{9,8},{10,11... | collective-permute-start | bytes 6291464 | tf_op jit(solution)/shard_map/ppermute | solution.py:40
  55.1 15.1 %collective-permute-start.10 = (bf16[512,512]{1,0:T(8,128)(2,1)}, bf16[512,512]{1,0:T(8,128)(2,1)}, u32[]{:S(2)}, u32[]{:S(2)}) collective-permute-start(bf16[512,512]{1,0:T(8,128)(2,1)} %collective-permute-done.7.refs_5_), channel_id=1, source_target_pairs={{0,224},{8,232},{16,240},{24,248},{32,0},{40,8},{48,16},{56,24},{6... | collective-permute-start | bytes 1572872 | tf_op jit(solution)/shard_map/ppermute | solution.py:32
  58.1 15.5 %collective-permute-start.13 = (bf16[512,512]{1,0:T(8,128)(2,1)}, bf16[512,512]{1,0:T(8,128)(2,1)}, u32[]{:S(2)}, u32[]{:S(2)}) collective-permute-start(bf16[512,512]{1,0:T(8,128)(2,1)} %collective-permute-done.8.refs_6_), channel_id=1, source_target_pairs={{0,32},{8,40},{16,48},{24,56},{32,64},{40,72},{48,80},{56,88},{64,... | collective-permute-start | bytes 1572872 | tf_op jit(solution)/shard_map/ppermute | solution.py:32
  61.8 11.8 %collective-permute-start.16 = (bf16[64,2048]{1,0:T(8,128)(2,1)S(1)}, bf16[64,2048]{1,0:T(8,128)(2,1)S(1)}, u32[]{:S(2)}, u32[]{:S(2)}) collective-permute-start(bf16[64,2048]{1,0:T(8,128)(2,1)S(1)} %get-tuple-element.23), channel_id=1, source_target_pairs={{0,8},{8,0},{16,24},{24,16},{32,40},{40,32},{48,56},{56,48},{64,72... | collective-permute-start | bytes 786440 | tf_op jit(solution)/shard_map/ppermute | solution.py:36
  63.1 12.6 %collective-permute-start.28 = (bf16[64,2048]{1,0:T(8,128)(2,1)S(1)}, bf16[64,2048]{1,0:T(8,128)(2,1)S(1)}, u32[]{:S(2)}, u32[]{:S(2)}) collective-permute-start(bf16[64,2048]{1,0:T(8,128)(2,1)S(1)} %get-tuple-element.27), channel_id=1, source_target_pairs={{0,16},{8,24},{16,0},{24,8},{32,48},{40,56},{48,32},{56,40},{64,80... | collective-permute-start | bytes 786440 | tf_op jit(solution)/shard_map/ppermute | solution.py:36
  73.6 9.2 %copy-start.15 = (bf16[64,2048]{1,0:T(8,128)(2,1)}, bf16[64,2048]{1,0:T(8,128)(2,1)S(1)}, u32[]{:S(2)}) copy-start(bf16[64,2048]{1,0:T(8,128)(2,1)S(1)} %collective-permute-done.16) | copy-start | bytes 786436
  75.7 7.1 %copy-start.16 = (bf16[64,2048]{1,0:T(8,128)(2,1)}, bf16[64,2048]{1,0:T(8,128)(2,1)S(1)}, u32[]{:S(2)}) copy-start(bf16[64,2048]{1,0:T(8,128)(2,1)S(1)} %collective-permute-done.28) | copy-start | bytes 786436
  75.7 10.2 %collective-permute-start.29 = (bf16[64,2048]{1,0:T(8,128)(2,1)S(1)}, bf16[64,2048]{1,0:T(8,128)(2,1)}, u32[]{:S(2)}, u32[]{:S(2)}) collective-permute-start(bf16[64,2048]{1,0:T(8,128)(2,1)S(1)} %get-tuple-element.27), channel_id=1, source_target_pairs={{0,24},{8,16},{16,8},{24,0},{32,56},{40,48},{48,40},{56,32},{64,88... | collective-permute-start | bytes 786440 | tf_op jit(solution)/shard_map/ppermute | solution.py:36
  79.6 13.3 %collective-permute-start.11 = (bf16[512,512]{1,0:T(8,128)(2,1)}, bf16[512,512]{1,0:T(8,128)(2,1)}, u32[]{:S(2)}, u32[]{:S(2)}) collective-permute-start(bf16[512,512]{1,0:T(8,128)(2,1)} %collective-permute-done.10.refs_4_), channel_id=1, source_target_pairs={{0,224},{8,232},{16,240},{24,248},{32,0},{40,8},{48,16},{56,24},{6... | collective-permute-start | bytes 1572872 | tf_op jit(solution)/shard_map/ppermute | solution.py:32
  82.5 14.0 %collective-permute-start.14 = (bf16[512,512]{1,0:T(8,128)(2,1)}, bf16[512,512]{1,0:T(8,128)(2,1)}, u32[]{:S(2)}, u32[]{:S(2)}) collective-permute-start(bf16[512,512]{1,0:T(8,128)(2,1)} %collective-permute-done.13.refs_5_), channel_id=1, source_target_pairs={{0,32},{8,40},{16,48},{24,56},{32,64},{40,72},{48,80},{56,88},{64,... | collective-permute-start | bytes 1572872 | tf_op jit(solution)/shard_map/ppermute | solution.py:32
  82.8 13.8 %collective-permute-start.17 = (bf16[512,512]{1,0:T(8,128)(2,1)}, bf16[512,512]{1,0:T(8,128)(2,1)S(1)}, u32[]{:S(2)}, u32[]{:S(2)}) collective-permute-start(bf16[512,512]{1,0:T(8,128)(2,1)} %get-tuple-element.30), channel_id=1, source_target_pairs={{0,8},{8,0},{16,24},{24,16},{32,40},{40,32},{48,56},{56,48},{64,72... | collective-permute-start | bytes 1572872 | tf_op jit(solution)/shard_map/ppermute | solution.py:36
  96.6 9.3 %copy-start.4 = (bf16[512,512]{1,0:T(8,128)(2,1)}, bf16[512,512]{1,0:T(8,128)(2,1)S(1)}, u32[]{:S(2)}) copy-start(bf16[512,512]{1,0:T(8,128)(2,1)S(1)} %collective-permute-done.17.refs_9_.right_1) | copy-start | bytes 1572868
  96.6 17.0 %collective-permute-start.30 = (bf16[192,2048]{1,0:T(8,128)(2,1)S(1)}, bf16[192,2048]{1,0:T(8,128)(2,1)S(1)}, u32[]{:S(2)}, u32[]{:S(2)}) collective-permute-start(bf16[192,2048]{1,0:T(8,128)(2,1)S(1)} %pad_maximum_fusion), channel_id=1, source_target_pairs={{0,6},{1,7},{2,0},{3,1},{4,2},{5,3},{6,4},{7,5},{8,14},{9,15},{10,... | collective-permute-start | bytes 2359304 | tf_op jit(solution)/shard_map/ppermute | solution.py:47
  97.2 17.9 %collective-permute-start.31 = (bf16[192,2048]{1,0:T(8,128)(2,1)S(1)}, bf16[192,2048]{1,0:T(8,128)(2,1)S(1)}, u32[]{:S(2)}, u32[]{:S(2)}) collective-permute-start(bf16[192,2048]{1,0:T(8,128)(2,1)S(1)} %pad_maximum_fusion), channel_id=1, source_target_pairs={{0,2},{1,3},{2,4},{3,5},{4,6},{5,7},{6,0},{7,1},{8,10},{9,11},{10,... | collective-permute-start | bytes 2359304 | tf_op jit(solution)/shard_map/ppermute | solution.py:47
  113.5 1.5 copy-start.12
  115.1 0.9 copy-start.10
  116.0 17.3 %collective-permute-start.32 = (bf16[192,2048]{1,0:T(8,128)(2,1)S(1)}, bf16[192,2048]{1,0:T(8,128)(2,1)S(1)}, u32[]{:S(2)}, u32[]{:S(2)}) collective-permute-start(bf16[192,2048]{1,0:T(8,128)(2,1)S(1)} %pad_maximum_fusion), channel_id=1, source_target_pairs={{0,4},{1,5},{2,6},{3,7},{4,0},{5,1},{6,2},{7,3},{8,12},{9,13},{10,... | collective-permute-start | bytes 2359304 | tf_op jit(solution)/shard_map/ppermute | solution.py:47
  116.5 16.8 %copy-start.11 = (bf16[192,2048]{1,0:T(8,128)(2,1)S(1)}, bf16[192,2048]{1,0:T(8,128)(2,1)}, u32[]{:S(2)}) copy-start(bf16[192,2048]{1,0:T(8,128)(2,1)} %copy-done.10) | copy-start | bytes 2359300
  116.6 17.0 %copy-start = (bf16[512,4096]{1,0:T(8,128)(2,1)S(1)}, bf16[512,4096]{1,0:T(8,128)(2,1)}, u32[]{:S(2)}) copy-start(bf16[512,4096]{1,0:T(8,128)(2,1)} %left.5) | copy-start | bytes 12582916
  133.4 11.0 %copy-start.18 = (f32[1024]{0:T(1024)S(1)}, f32[1024]{0:T(1024)}, u32[]{:S(2)}) copy-start(f32[1024]{0:T(1024)} %param.9) | copy-start | bytes 12292
  133.4 69.7 %collective-permute-start.33 = (bf16[768,2048]{1,0:T(8,128)(2,1)S(1)}, bf16[768,2048]{1,0:T(8,128)(2,1)}, u32[]{:S(2)}, u32[]{:S(2)}) collective-permute-start(bf16[768,2048]{1,0:T(8,128)(2,1)S(1)} %constant_dynamic-update-slice_fusion.4.line), channel_id=1, source_target_pairs={{0,1},{1,0},{2,3},{3,2},{4,5},{5,4},{6,7},{7,6},{8,9},{9,8},{10,11... | collective-permute-start | bytes 9437192 | tf_op jit(solution)/shard_map/ppermute | solution.py:40
  137.0 45.4 %collective-permute-start.34 = (bf16[512,512]{1,0:T(8,128)(2,1)}, bf16[512,512]{1,0:T(8,128)(2,1)}, u32[]{:S(2)}, u32[]{:S(2)}) collective-permute-start(bf16[512,512]{1,0:T(8,128)(2,1)} %get-tuple-element.30), channel_id=1, source_target_pairs={{0,24},{8,16},{16,8},{24,0},{32,56},{40,48},{48,40},{56,32},{64,88... | collective-permute-start | bytes 1572872 | tf_op jit(solution)/shard_map/ppermute | solution.py:36
  138.5 8.5 %collective-permute-start.12 = (bf16[256,512]{1,0:T(8,128)(2,1)S(1)}, bf16[256,512]{1,0:T(8,128)(2,1)S(1)}, u32[]{:S(2)}, u32[]{:S(2)}) collective-permute-start(bf16[256,512]{1,0:T(8,128)(2,1)S(1)} %slice.68), channel_id=1, source_target_pairs={{0,224},{8,232},{16,240},{24,248},{32,0},{40,8},{48,16},{56,24},{6... | collective-permute-start | bytes 786440 | tf_op jit(solution)/shard_map/ppermute | solution.py:32
  141.7 9.7 %collective-permute-start.15 = (bf16[256,512]{1,0:T(8,128)(2,1)S(1)}, bf16[256,512]{1,0:T(8,128)(2,1)S(1)}, u32[]{:S(2)}, u32[]{:S(2)}) collective-permute-start(bf16[256,512]{1,0:T(8,128)(2,1)S(1)} %slice.69), channel_id=1, source_target_pairs={{0,32},{8,40},{16,48},{24,56},{32,64},{40,72},{48,80},{56,88},{64,... | collective-permute-start | bytes 786440 | tf_op jit(solution)/shard_map/ppermute | solution.py:32
  141.8 4.1 %collective-permute-start.18 = (f32[4,128]{1,0:T(4,128)S(1)}, f32[4,128]{1,0:T(4,128)S(1)}, u32[]{:S(2)}, u32[]{:S(2)}) collective-permute-start(f32[4,128]{1,0:T(4,128)S(1)} %multiply_bitcast_fusion), channel_id=1, source_target_pairs={{0,8},{8,0},{16,24},{24,16},{32,40},{40,32},{48,56},{56,48},{64,72... | collective-permute-start | bytes 6152 | tf_op jit(solution)/shard_map/ppermute | solution.py:36
  147.0 5.1 %copy-start.13 = (bf16[256,512]{1,0:T(8,128)(2,1)}, bf16[256,512]{1,0:T(8,128)(2,1)S(1)}, u32[]{:S(2)}) copy-start(bf16[256,512]{1,0:T(8,128)(2,1)S(1)} %collective-permute-done.12.refs_4_) | copy-start | bytes 786436
  151.4 0.7 copy-start.14
  152.2 26.1 %copy-start.17 = (s32[512]{0:T(512)S(1)}, s32[512]{0:T(512)}, u32[]{:S(2)}) copy-start(s32[512]{0:T(512)} %param.10) | copy-start | bytes 6148
  152.2 30.3 %copy-start.3 = (bf16[512,512]{1,0:T(8,128)(2,1)S(1)}, bf16[512,512]{1,0:T(8,128)(2,1)}, u32[]{:S(2)}) copy-start(bf16[512,512]{1,0:T(8,128)(2,1)} %get-tuple-element.31.refs_8_.right) | copy-start | bytes 1572868
  152.2 50.9 %copy-start.6 = (s32[4]{0:T(128)S(1)}, s32[4]{0:T(128)}, u32[]{:S(2)}) copy-start(s32[4]{0:T(128)} %pad_add_fusion.refs_0_.place) | copy-start | bytes 52
  157.1 11.7 %collective-permute-start.19 = (f32[8,128]{1,0:T(8,128)}, f32[8,128]{1,0:T(8,128)S(1)}, u32[]{:S(2)}, u32[]{:S(2)}) collective-permute-start(f32[8,128]{1,0:T(8,128)} %shard_map.95), channel_id=1, source_target_pairs={{0,1},{1,0},{2,3},{3,2},{4,5},{5,4},{6,7},{7,6},{8,9},{9,8},{10,11... | collective-permute-start | bytes 12296 | tf_op jit(solution)/shard_map/ppermute | solution.py:40
  169.5 3.6 %collective-permute-start.20 = (f32[8,128]{1,0:T(8,128)S(1)}, f32[8,128]{1,0:T(8,128)S(1)}, u32[]{:S(2)}, u32[]{:S(2)}) collective-permute-start(f32[8,128]{1,0:T(8,128)S(1)} %add.131), channel_id=1, source_target_pairs={{0,2},{1,3},{2,0},{3,1},{4,6},{5,7},{6,4},{7,5},{8,10},{9,11},{10,... | collective-permute-start | bytes 12296 | tf_op jit(solution)/shard_map/ppermute | solution.py:40
  173.1 5.1 %collective-permute-start.21 = (f32[8,128]{1,0:T(8,128)S(1)}, f32[8,128]{1,0:T(8,128)S(1)}, u32[]{:S(2)}, u32[]{:S(2)}) collective-permute-start(f32[8,128]{1,0:T(8,128)S(1)} %add.132), channel_id=1, source_target_pairs={{0,4},{1,5},{2,6},{3,7},{4,0},{5,1},{6,2},{7,3},{8,12},{9,13},{10,... | collective-permute-start | bytes 12296 | tf_op jit(solution)/shard_map/ppermute | solution.py:40
  178.3 7.2 %collective-permute-start.22 = (f32[8,128]{1,0:T(8,128)S(1)}, f32[8,128]{1,0:T(8,128)S(1)}, u32[]{:S(2)}, u32[]{:S(2)}) collective-permute-start(f32[8,128]{1,0:T(8,128)S(1)} %pad_maximum_fusion.4), channel_id=1, source_target_pairs={{0,8},{8,0},{16,24},{24,16},{32,40},{40,32},{48,56},{56,48},{64,72... | collective-permute-start | bytes 12296 | tf_op jit(solution)/shard_map/ppermute | solution.py:36
  179.9 5.5 %collective-permute-start.24 = (f32[8,128]{1,0:T(8,128)S(1)}, f32[8,128]{1,0:T(8,128)S(1)}, u32[]{:S(2)}, u32[]{:S(2)}) collective-permute-start(f32[8,128]{1,0:T(8,128)S(1)} %pad_maximum_fusion.4), channel_id=1, source_target_pairs={{0,24},{8,16},{16,8},{24,0},{32,56},{40,48},{48,40},{56,32},{64,88... | collective-permute-start | bytes 12296 | tf_op jit(solution)/shard_map/ppermute | solution.py:36
  181.9 5.2 %collective-permute-start.23 = (f32[8,128]{1,0:T(8,128)S(1)}, f32[8,128]{1,0:T(8,128)S(1)}, u32[]{:S(2)}, u32[]{:S(2)}) collective-permute-start(f32[8,128]{1,0:T(8,128)S(1)} %pad_maximum_fusion.4), channel_id=1, source_target_pairs={{0,16},{8,24},{16,0},{24,8},{32,48},{40,56},{48,32},{56,40},{64,80... | collective-permute-start | bytes 12296 | tf_op jit(solution)/shard_map/ppermute | solution.py:36
  182.5 20.6 %collective-permute-start.35 = (bf16[512,512]{1,0:T(8,128)(2,1)S(1)}, bf16[512,512]{1,0:T(8,128)(2,1)S(1)}, u32[]{:S(2)}, u32[]{:S(2)}) collective-permute-start(bf16[512,512]{1,0:T(8,128)(2,1)S(1)} %copy-done.3), channel_id=1, source_target_pairs={{0,16},{8,24},{16,0},{24,8},{32,48},{40,56},{48,32},{56,40},{64,80... | collective-permute-start | bytes 1572872 | tf_op jit(solution)/shard_map/ppermute | solution.py:36
  187.1 3.7 %collective-permute-start.25 = (f32[8,128]{1,0:T(8,128)S(1)}, f32[8,128]{1,0:T(8,128)S(1)}, u32[]{:S(2)}, u32[]{:S(2)}) collective-permute-start(f32[8,128]{1,0:T(8,128)S(1)} %pad_maximum_fusion.5), channel_id=1, source_target_pairs={{0,32},{8,40},{16,48},{24,56},{32,0},{40,8},{48,16},{56,24},{64,96... | collective-permute-start | bytes 12296 | tf_op jit(solution)/shard_map/ppermute | solution.py:36
  190.9 4.6 %collective-permute-start.26 = (f32[8,128]{1,0:T(8,128)S(1)}, f32[8,128]{1,0:T(8,128)S(1)}, u32[]{:S(2)}, u32[]{:S(2)}) collective-permute-start(f32[8,128]{1,0:T(8,128)S(1)} %fusion.15), channel_id=1, source_target_pairs={{0,64},{8,72},{16,80},{24,88},{32,96},{40,104},{48,112},{56,120},{... | collective-permute-start | bytes 12296 | tf_op jit(solution)/shard_map/ppermute | solution.py:36
  195.5 7.6 %collective-permute-start.27 = (f32[8,128]{1,0:T(8,128)S(1)}, f32[8,128]{1,0:T(8,128)S(1)}, u32[]{:S(2)}, u32[]{:S(2)}) collective-permute-start(f32[8,128]{1,0:T(8,128)S(1)} %add.146), channel_id=1, source_target_pairs={{0,128},{8,136},{16,144},{24,152},{32,160},{40,168},{48,176},{56,1... | collective-permute-start | bytes 12296 | tf_op jit(solution)/shard_map/ppermute | solution.py:36
  203.1 1.0 copy-start.5
  204.1 7.1 %copy-start.1 = (bf16[512,4096]{1,0:T(8,128)(2,1)S(1)}, bf16[512,4096]{1,0:T(8,128)(2,1)}, u32[]{:S(2)}) copy-start(bf16[512,4096]{1,0:T(8,128)(2,1)} %left.5) | copy-start | bytes 12582916
  208.0 6.9 %collective-permute-start.36 = (bf16[256,256]{1,0:T(8,128)(2,1)S(1)}, bf16[256,256]{1,0:T(8,128)(2,1)S(1)}, u32[]{:S(2)}, u32[]{:S(2)}) collective-permute-start(bf16[256,256]{1,0:T(8,128)(2,1)S(1)} %get-tuple-element.36), channel_id=1, source_target_pairs={{0,32},{8,40},{16,48},{24,56},{32,64},{40,72},{48,80},{56,88},{64,... | collective-permute-start | bytes 393224 | tf_op jit(solution)/shard_map/ppermute | solution.py:32
  208.0 6.9 %collective-permute-start.40 = (bf16[256,256]{1,0:T(8,128)(2,1)S(1)}, bf16[256,256]{1,0:T(8,128)(2,1)S(1)}, u32[]{:S(2)}, u32[]{:S(2)}) collective-permute-start(bf16[256,256]{1,0:T(8,128)(2,1)S(1)} %get-tuple-element.37), channel_id=1, source_target_pairs={{0,224},{8,232},{16,240},{24,248},{32,0},{40,8},{48,16},{56,24},{6... | collective-permute-start | bytes 393224 | tf_op jit(solution)/shard_map/ppermute | solution.py:32
  215.0 10.4 %collective-permute-start.37 = (bf16[256,512]{1,0:T(8,128)(2,1)S(1)}, bf16[256,512]{1,0:T(8,128)(2,1)S(1)}, u32[]{:S(2)}, u32[]{:S(2)}) collective-permute-start(bf16[256,512]{1,0:T(8,128)(2,1)S(1)} %get-tuple-element.48), channel_id=1, source_target_pairs={{0,32},{8,40},{16,48},{24,56},{32,64},{40,72},{48,80},{56,88},{64,... | collective-permute-start | bytes 786440 | tf_op jit(solution)/shard_map/ppermute | solution.py:32
  221.3 20.5 %copy-start.2 = (f32[5,256,512]{2,1,0:T(8,128)}, f32[5,256,512]{2,1,0:T(8,128)S(1)}, u32[]{:S(2)}) copy-start(f32[5,256,512]{2,1,0:T(8,128)S(1)} %shard_map.97) | copy-start | bytes 7864324
  221.3 9.7 %collective-permute-start.41 = (bf16[256,512]{1,0:T(8,128)(2,1)S(1)}, bf16[256,512]{1,0:T(8,128)(2,1)S(1)}, u32[]{:S(2)}, u32[]{:S(2)}) collective-permute-start(bf16[256,512]{1,0:T(8,128)(2,1)S(1)} %get-tuple-element.49), channel_id=1, source_target_pairs={{0,224},{8,232},{16,240},{24,248},{32,0},{40,8},{48,16},{56,24},{6... | collective-permute-start | bytes 786440 | tf_op jit(solution)/shard_map/ppermute | solution.py:32
  225.5 29.2 %copy-start.8 = (f32[128,1024]{1,0:T(8,128)S(1)}, f32[128,1024]{1,0:T(8,128)}, u32[]{:S(2)}) copy-start(f32[128,1024]{1,0:T(8,128)} %param.11) | copy-start | bytes 1572868
  225.5 9.7 %collective-permute-start.38 = (bf16[256,512]{1,0:T(8,128)(2,1)S(1)}, bf16[256,512]{1,0:T(8,128)(2,1)S(1)}, u32[]{:S(2)}, u32[]{:S(2)}) collective-permute-start(bf16[256,512]{1,0:T(8,128)(2,1)S(1)} %fusion.9), channel_id=1, source_target_pairs={{0,32},{8,40},{16,48},{24,56},{32,64},{40,72},{48,80},{56,88},{64,... | collective-permute-start | bytes 786440 | tf_op jit(solution)/shard_map/ppermute | solution.py:32
  235.3 6.4 %collective-permute-start.42 = (bf16[256,512]{1,0:T(8,128)(2,1)S(1)}, bf16[256,512]{1,0:T(8,128)(2,1)S(1)}, u32[]{:S(2)}, u32[]{:S(2)}) collective-permute-start(bf16[256,512]{1,0:T(8,128)(2,1)S(1)} %get-tuple-element.47), channel_id=1, source_target_pairs={{0,224},{8,232},{16,240},{24,248},{32,0},{40,8},{48,16},{56,24},{6... | collective-permute-start | bytes 786440 | tf_op jit(solution)/shard_map/ppermute | solution.py:32
  235.4 9.1 %collective-permute-start.39 = (bf16[256,512]{1,0:T(8,128)(2,1)S(1)}, bf16[256,512]{1,0:T(8,128)(2,1)S(1)}, u32[]{:S(2)}, u32[]{:S(2)}) collective-permute-start(bf16[256,512]{1,0:T(8,128)(2,1)S(1)} %get-tuple-element.46), channel_id=1, source_target_pairs={{0,32},{8,40},{16,48},{24,56},{32,64},{40,72},{48,80},{56,88},{64,... | collective-permute-start | bytes 786440 | tf_op jit(solution)/shard_map/ppermute | solution.py:32
  241.9 6.5 %collective-permute-start.43 = (bf16[256,512]{1,0:T(8,128)(2,1)S(1)}, bf16[256,512]{1,0:T(8,128)(2,1)S(1)}, u32[]{:S(2)}, u32[]{:S(2)}) collective-permute-start(bf16[256,512]{1,0:T(8,128)(2,1)S(1)} %fusion.5), channel_id=1, source_target_pairs={{0,224},{8,232},{16,240},{24,248},{32,0},{40,8},{48,16},{56,24},{6... | collective-permute-start | bytes 786440 | tf_op jit(solution)/shard_map/ppermute | solution.py:32
  249.6 5.1 %collective-permute-start.44 = (bf16[128,512]{1,0:T(8,128)(2,1)S(1)}, bf16[128,512]{1,0:T(8,128)(2,1)S(1)}, u32[]{:S(2)}, u32[]{:S(2)}) collective-permute-start(bf16[128,512]{1,0:T(8,128)(2,1)S(1)} %fusion.14), channel_id=1, source_target_pairs={{0,8},{8,0},{16,24},{24,16},{32,40},{40,32},{48,56},{56,48},{64,72... | collective-permute-start | bytes 393224 | tf_op jit(solution)/shard_map/ppermute | solution.py:36

commit v2 on v0

v2 whole, which is shorter than its diff:
```python
import math

import jax
import jax.numpy as jnp
from jax import lax
from jax.experimental import pallas as pl
from jax.experimental.pallas import tpu as pltpu
from jax.sharding import PartitionSpec as P

D = 4096
F = 8192
NZ, NY, NX = 8, 4, 4
MEMBERS = 512
POPULATION = MEMBERS * NZ * NY
OTHERS = 3 * MEMBERS
SHARE = 64

noise_scale = 0.5
learn_rate = 0.01
epsilon = 1e-05

bf16 = jnp.bfloat16
f32 = jnp.float32


def move(value, dz, dy):
    pairs = [
        (z * NY + y, (z + dz) % NZ * NY + (y + dy) % NY)
        for z in range(NZ)
        for y in range(NY)
    ]
    return lax.ppermute(value, "pop", pairs)


def swap_pop(value, mask):
    return lax.ppermute(value, "pop", [(i, i ^ mask) for i in range(NZ * NY)])


def swap_wa(value, mask):
    return lax.ppermute(value, "wa", [(i, i ^ mask) for i in range(2 * NX)])


def after(value, *others):
    return lax.optimization_barrier((value, *others))[0]


def load_pieces(z, plan, sources, pieces, gathered, weights, arrived):
    copies, at = [], 0
    for (dz, depth), piece in zip(plan, pieces):
        here = pl.ds(at, depth)
        columns = pl.ds(pl.multiple_of(lax.rem(z + dz, NZ) * 512, 512), depth)
        moves = [(piece, weights.at[here, :])]
        for index, source in enumerate(sources):
            rows = pl.ds(index * MEMBERS, MEMBERS)
            moves.append((source.at[:, columns], gathered.at[rows, here]))
        for source, target in moves:
            copies.append(pltpu.make_async_copy(source, target, arrived.at[len(copies)]))
            copies[-1].start()
        at += depth
    return copies


def forward_kernel(plan, has_total, place, source, *refs):
    pieces = refs[: len(plan)]
    total_in = refs[len(plan)] if has_total else None
    out, weights, gathered, arrived = refs[-4:]
    copies = load_pieces(place[0], plan, [source], pieces, gathered, weights, arrived)
    cut = len(plan) // 2 if len(plan) > 4 else len(plan)
    for first, last in ((0, cut), (cut, len(plan))):
        if first == last:
            continue
        for copy in copies[2 * first : 2 * last]:
            copy.wait()
        for row in range(0, MEMBERS, 256):
            rows = pl.ds(row, 256)
            term = jnp.dot(
                gathered[rows, first * 512 : last * 512],
                weights[first * 512 : last * 512, :],
                preferred_element_type=f32,
            )
            if first:
                term = term + out[rows, :]
            elif has_total:
                term = term + total_in[rows, :]
            out[rows, :] = term


def forward(place, source, pieces, total=None):
    plan = tuple((dz, 512) for dz, _ in pieces)
    depth = 512 * len(plan)
    vmem, hbm = pl.BlockSpec(memory_space=pltpu.VMEM), pl.BlockSpec(memory_space=pl.ANY)
    totals = [] if total is None else [total]
    return pl.pallas_call(
        lambda *refs: forward_kernel(plan, total is not None, *refs),
        in_specs=[pl.BlockSpec(memory_space=pltpu.SMEM)]
        + [hbm] * (1 + len(pieces))
        + [vmem] * len(totals),
        out_specs=vmem,
        out_shape=jax.ShapeDtypeStruct((MEMBERS, 512), f32),
        scratch_shapes=[
            pltpu.VMEM((depth, 512), bf16),
            pltpu.VMEM((MEMBERS, depth), bf16),
            pltpu.SemaphoreType.DMA((2 * len(plan),)),
        ],
        compiler_params=pltpu.CompilerParams(vmem_limit_bytes=60 * 2**20),
        cost_estimate=pl.CostEstimate(
            flops=2 * MEMBERS * depth * 512,
            bytes_accessed=depth * 2 * 1024 + 2 * 2**20,
            transcendentals=0,
        ),
    )(place, source, *[piece for _, piece in pieces], *totals)


def reward_kernel(plan, place, inputs, partner, *refs):
    pieces, refs = refs[: len(plan)], refs[len(plan) :]
    own, other, projected, right, right_1, probe, out, weights, gathered, arrived = refs
    copies = load_pieces(
        place[0], plan, [inputs, partner], pieces, gathered, weights, arrived
    )
    first = pl.multiple_of(place[1] * 512, 512)
    for copy in copies:
        copy.wait()
    for group in range(2 * MEMBERS // 128):
        mine = group < MEMBERS // 128
        total, noise = (own, right) if mine else (other, right_1)
        rows = pl.ds(group % (MEMBERS // 128) * 128, 128)
        outputs = total[rows, :] + jnp.dot(
            gathered[group * 128 : (group + 1) * 128, :],
            weights[...],
            preferred_element_type=f32,
        )
        wide = noise_scale * jnp.transpose(
            jnp.broadcast_to(projected[group : group + 1, :], (128, 128))
        )
        terms = jnp.zeros((128, 128), f32)
        for lane in range(0, 512, 128):
            drawn = noise[rows, pl.ds(pl.multiple_of(first + lane, 128), 128)].astype(f32)
            lanes = outputs[:, lane : lane + 128] + wide * drawn
            terms = terms + jnp.tanh(lanes) * probe[:, lane : lane + 128]
        out[pl.ds(group, 1), :] = jnp.sum(
            jnp.transpose(terms), axis=0, keepdims=True
        ) / math.sqrt(F)


def reward_terms(place, inputs, partner, pieces, *operands):
    plan = tuple((dz, 512) for dz, _ in pieces)
    depth = 512 * len(plan)
    vmem, hbm = pl.BlockSpec(memory_space=pltpu.VMEM), pl.BlockSpec(memory_space=pl.ANY)
    return pl.pallas_call(
        lambda *refs: reward_kernel(plan, *refs),
        in_specs=[pl.BlockSpec(memory_space=pltpu.SMEM)]
        + [hbm] * (2 + len(plan))
        + [vmem] * len(operands),
        out_specs=vmem,
        out_shape=jax.ShapeDtypeStruct((8, 128), f32),
        scratch_shapes=[
            pltpu.VMEM((depth, 512), bf16),
            pltpu.VMEM((2 * MEMBERS, depth), bf16),
            pltpu.SemaphoreType.DMA((3 * len(plan),)),
        ],
        compiler_params=pltpu.CompilerParams(vmem_limit_bytes=60 * 2**20),
        cost_estimate=pl.CostEstimate(
            flops=4 * MEMBERS * depth * 512, bytes_accessed=6 * 2**20, transcendentals=0
        ),
    )(place, inputs, partner, *[piece for _, piece in pieces], *operands)


def update_dot(left, right):
    return lax.dot_general(
        left, right, (((0,), (0,)), ((), ())), preferred_element_type=f32
    )


def plane_sum(count, lefts, lines, right, right_line):
    left = jnp.concatenate([ref[...] for ref in lefts], axis=1)
    line = jnp.concatenate([ref[...] for ref in lines], axis=1)
    return update_dot(left, right[...]) + update_dot(line, right_line[...])


def update_kernel(count, place, *refs):
    lefts, lines = refs[:count], refs[count : 2 * count]
    right, right_line, out = refs[2 * count :]
    total = plane_sum(count, lefts, lines, right, right_line)
    for index in range(count):
        out[index] = total[index * 128 : (index + 1) * 128]


def first_kernel(place, sums, left, line, raw, right, right_1, right_2, right_3, *outs):
    up, down, fitness, scaled, scaled_line = outs

    def total_of(tile):
        return jnp.sum(jnp.sum(tile, axis=1, keepdims=True), axis=0, keepdims=True)

    center = total_of(sums[:4, :]) / POPULATION
    spread = total_of(sums[4:, :]) / POPULATION - center * center
    scale = lax.rsqrt(spread + epsilon)
    fitness[...] = (raw[:4, :] - center) * scale

    def wide(row):
        fit = (raw[row : row + 1, :] - center) * scale / math.sqrt(POPULATION)
        return jnp.transpose(jnp.broadcast_to(fit, (128, 128)))

    def store(target, at, fit, values, row):
        count = fit.shape[0]
        for lane in range(0, 1024, 128):
            drawn = values[row : row + count, lane : lane + 128].astype(f32)
            target[at : at + count, lane : lane + 128] = (fit * drawn).astype(bf16)

    for row in range(4):
        store(scaled, row * 128, wide(row), right, row * 128)
    for index, values in enumerate((right_1, right_2, right_3)):
        for row in range(4):
            fit = wide(4 * index + 4 + row)
            for side in range(2):
                owner = 2 * row + side
                part = fit[side * SHARE : (side + 1) * SHARE]
                store(scaled_line, (3 * owner + index) * SHARE, part, values, owner * SHARE)
    total = plane_sum(1, [left], [line], scaled, scaled_line)
    up[...] = total[:, :512].astype(bf16)
    down[...] = total[:, 512:].astype(bf16)


def left_specs(distances):
    def of(rows, turn):
        return [
            pl.BlockSpec((rows, 128), lambda i, s, dz=dz: (0, turn(lax.rem(s[0] + dz, NZ), s)))
            for dz in distances
        ]

    return of(MEMBERS, lambda z, s: z * NY + s[2]) + of(OTHERS, lambda z, s: z)


def whole(shape):
    return pl.BlockSpec(shape, lambda i, s: (0,) * len(shape))


def update_first(place, sums, left, line, raw, rights):
    shapes = [(MEMBERS, 1024), (OTHERS, 1024)]
    return pl.pallas_call(
        first_kernel,
        grid_spec=pltpu.PrefetchScalarGridSpec(
            num_scalar_prefetch=1,
            grid=(1,),
            in_specs=[whole((8, 128))]
            + left_specs((4,))
            + [whole((16, 128))]
            + [whole((MEMBERS, 1024))] * 4,
            out_specs=[whole((128, 512))] * 2
            + [whole((4, 128))]
            + [whole(shape) for shape in shapes],
        ),
        out_shape=[jax.ShapeDtypeStruct((128, 512), bf16)] * 2
        + [jax.ShapeDtypeStruct((4, 128), f32)]
        + [jax.ShapeDtypeStruct(shape, bf16) for shape in shapes],
        compiler_params=pltpu.CompilerParams(vmem_limit_bytes=40 * 2**20),
        cost_estimate=pl.CostEstimate(
            flops=2 * 2048 * 256 * 512, bytes_accessed=6 * 2**20, transcendentals=0
        ),
    )(place, sums, left, line, raw, *rights)


def update_rest(place, left, line, right, right_line, distances):
    count = len(distances)
    return pl.pallas_call(
        lambda *refs: update_kernel(count, *refs),
        grid_spec=pltpu.PrefetchScalarGridSpec(
            num_scalar_prefetch=1,
            grid=(1,),
            in_specs=left_specs(distances) + [whole((MEMBERS, 1024)), whole((OTHERS, 1024))],
            out_specs=pl.BlockSpec((count, 128, 1024), lambda i, s: (0, 0, 0)),
        ),
        out_shape=jax.ShapeDtypeStruct((count, 128, 1024), f32),
        compiler_params=pltpu.CompilerParams(vmem_limit_bytes=40 * 2**20),
        cost_estimate=pl.CostEstimate(
            flops=2 * 2048 * 256 * 512, bytes_accessed=2**20, transcendentals=0
        ),
    )(place, *[left] * count, *[line] * count, right, right_line)


def shards(inputs, noise_left, noise_right, reward_probe, scores, master):
    pop, wa = lax.axis_index("pop"), lax.axis_index("wa")
    z, y = pop // NY, pop % NY
    half, parity = y // 2, y % 2
    place = jnp.stack([z, parity, y]).astype(jnp.int32)

    weight = master.astype(bf16)
    weight_own = lax.dynamic_slice_in_dim(weight, parity * 512, 512, 1)
    weight_not = lax.dynamic_slice_in_dim(weight, (1 - parity) * 512, 512, 1)
    rel = [
        weight_own,
        swap_pop(weight_not, 1),
        swap_pop(weight_own, 2),
        swap_pop(weight_not, 3),
    ]
    odd, high = parity == 1, half == 1
    rel = [jnp.where(odd, rel[i ^ 1], rel[i]) for i in range(NY)]
    whole_y = jnp.concatenate([jnp.where(high, rel[i ^ 2], rel[i]) for i in range(NY)])

    up1, down1 = move(whole_y, -1, 0), move(whole_y, 1, 0)
    share = lax.dynamic_slice_in_dim(inputs, wa * SHARE, SHARE, 0)
    share = swap_pop(after(share, whole_y), 1)
    partner = lax.all_gather(after(share, up1, down1), "wa", axis=0, tiled=True)
    left_share = lax.dynamic_slice_in_dim(noise_left, wa * SHARE, SHARE, 0)
    left_share = jnp.swapaxes(left_share.reshape(SHARE, NZ, NY, 128), 0, 2).swapaxes(1, 2)
    left_share = left_share.reshape(NY, SHARE, D // NY)
    left_share = [
        lax.dynamic_index_in_dim(left_share, y ^ mask, 0, keepdims=False) for mask in (1, 2, 3)
    ]
    projected = jnp.sum(inputs.astype(f32) * noise_left.astype(f32), axis=1) / math.sqrt(D)
    projected = projected.reshape(4, 128)
    right_3 = swap_pop(after(noise_right, whole_y, projected), 3)

    up1, down1 = lax.optimization_barrier((up1, down1))
    up2, down2 = move(up1, -1, 0), move(down1, 1, 0)
    projected = jnp.concatenate([projected, swap_pop(after(projected, up1), 1)])
    right_1 = swap_pop(after(noise_right, up1, projected), 1)
    total = forward(place, inputs, [(0, whole_y), (1, up1), (7, down1)])

    up2, down2, right_3, projected = lax.optimization_barrier(
        (up2, down2, right_3, projected)
    )
    up3, down3 = move(up2, -1, 0), move(down2, 1, 0)
    total = forward(place, inputs, [(2, up2), (6, down2)], total)

    up3, down3, total, right_1 = lax.optimization_barrier((up3, down3, total, right_1))
    far = move(up3, -1, 0)
    fetched = jnp.concatenate(
        [swap_pop(after(left_share[mask - 1], up3), mask) for mask in (1, 2, 3)]
    )
    right_2 = swap_pop(after(noise_right, up3), 2)
    other = forward(
        place, partner, [(0, whole_y), (1, up1), (7, down1), (2, up2), (6, down2)]
    )
    line = lax.all_gather(after(fetched, partner, far), "wa", axis=0, tiled=True)
    probe = lax.dynamic_slice_in_dim(reward_probe, parity * 512, 512, 0).reshape(1, 512)
    reward = reward_terms(
        place,
        inputs,
        partner,
        [(3, up3), (5, down3), (4, far)],
        total,
        other,
        projected,
        noise_right,
        right_1,
        probe,
    )

    reward = reward + swap_wa(reward, 1)
    pair = [swap_wa(reward, mask) for mask in (2, 4, 6)]
    reward = after((reward + pair[0]) + (pair[1] + pair[2]), right_2)
    own = reward[:4] + scores.astype(f32).reshape(4, 128) / 16.0
    reward = jnp.concatenate([own, reward[4:]])
    others = [swap_pop(reward, mask) for mask in (1, 2, 3)]
    raw = [
        own + others[0][4:],
        reward[4:] + others[0][:4],
        others[1][:4] + others[2][4:],
        others[1][4:] + others[2][:4],
    ]
    sums = jnp.concatenate(
        [raw[0] + raw[1] + raw[2] + raw[3], sum(tile * tile for tile in raw)]
    )
    sums = sums + move(sums, 1, 0) + move(sums, -1, 0) + move(sums, 2, 0)
    sums = sums + move(sums, 4, 0)

    up, down, fitness, *scaled = update_first(
        place,
        sums,
        noise_left,
        line,
        jnp.concatenate(raw),
        (noise_right, right_1, right_2, right_3),
    )
    up = move(up, 1, 0).astype(f32)
    down = move(down, -1, 0).astype(f32)
    none = jnp.zeros((128, 512), f32)
    up = jnp.concatenate([up, none], axis=1)
    down = jnp.concatenate([none, down], axis=1)
    for distances in ((3, 5), (2, 6), (1, 7, 0)):
        parts = update_rest(place, noise_left, line, *scaled, distances)
        up = move((parts[0] + up).astype(bf16), 1, 0).astype(f32)
        down = move((parts[1] + down).astype(bf16), -1, 0).astype(f32)
    update = parts[2] + up + down
    new_master = master + learn_rate * update
    return (fitness.reshape(MEMBERS), update, new_master, new_master.astype(bf16))


def solution(mesh):
    return jax.shard_map(
        shards,
        mesh=mesh,
        in_specs=(
            P("pop", None),
            P("pop", None),
            P("pop", "wa"),
            P("wa"),
            P("pop"),
            P("pop", "wa"),
        ),
        out_specs=(P("pop"), P("pop", "wa"), P("pop", "wa"), P("pop", "wa")),
        check_vma=False,
    )
```

time: 477 us -> 201 us (0.42)
  waiting for transfers between devices: 340 us -> 68.3 us
  blocking collectives: 83.3 us -> 0 us
  starting transfers between devices: 0.08 us -> 69.1 us
  Pallas kernels: 0 us -> 31.7 us
  matrix products: 20.7 us -> 0 us
    reduce_scatter x1 -> x0, waiting for transfers between devices: 243 us -> none  [shards(): lax.psum_scatter(lax.dot_general(noise_left, scaled, dims, preferred_elem...]
    all_gather x1 -> x2, waiting for transfers between devices: 97.2 us -> 0.01 us  [the longest x1 0.01 us: shards(): partner = lax.all_gather(after(share, up1, down1), 'wa', axis=0, tiled=True)]
    psum x2 -> x0, blocking collectives: 83.3 us -> none  [the longest x1 69.2 us: shards(): lax.psum((jnp.sum(raw_fitness), jnp.sum(raw_fitness * raw_fitness)), 'pop')]
    ppermute x0 -> x37, starting transfers between devices: none -> 69.1 us  [the longest x19 30.9 us: move(): return lax.ppermute(value, 'pop', pairs)]
    ppermute x0 -> x37, waiting for transfers between devices: none -> 68.3 us  [the longest x19 43.3 us: move(): return lax.ppermute(value, 'pop', pairs)]
    pallas_call x0 -> x8, Pallas kernels: none -> 31.7 us  [the longest x3 14.2 us: forward(): pl.pallas_call(lambda *refs: forward_kernel(plan, total is not None, *ref...]
    dot_general x3 -> x0, matrix products: 20.7 us -> none  [the longest x1 10.4 us: shards(): lax.dot_general(noise_left, scaled, dims, preferred_element_type=jnp.floa...]
  transfers between devices with their start and end apart: 2 -> 39, of which waited for: 2 -> 24; matrix products, arithmetic and copies ran while one was open for 1% -> 5% of each run, Pallas kernels for 0% -> 14%
where the time goes in v2:
time: 201 us; the launch traced here: 199 us
  starting transfers between devices  69.1 us (34%)
  waiting for transfers between devices  68.3 us (34%)
  Pallas kernels  31.7 us (16%)
  between operations  14.5 us (7%)
  other arithmetic  10.2 us (5%)
  local copies, waits for them, and re-layouts  5.35 us (3%)
    ppermute x19, waiting for transfers between devices, move(): return lax.ppermute(value, 'pop', pairs)  43.3 us
    ppermute x19, starting transfers between devices, move(): return lax.ppermute(value, 'pop', pairs)  30.9 us
    ppermute x14, starting transfers between devices, swap_pop(): return lax.ppermute(value, 'pop', [(i, i ^ mask) for i in range(NZ * NY)])  22.8 us
    ppermute x14, waiting for transfers between devices, swap_pop(): return lax.ppermute(value, 'pop', [(i, i ^ mask) for i in range(NZ * NY)])  19.3 us
    ppermute x4, starting transfers between devices, swap_wa(): return lax.ppermute(value, 'wa', [(i, i ^ mask) for i in range(2 * NX)])  15.3 us
    pallas_call x3, Pallas kernels, forward(): pl.pallas_call(lambda *refs: forward_kernel(plan, total is not None, *ref...  14.2 us
    pallas_call x1, Pallas kernels, reward_terms(): pl.pallas_call(lambda *refs: reward_kernel(plan, *refs), in_specs=[pl.Blo...  7.31 us
    pallas_call x3, Pallas kernels, update_rest(): pl.pallas_call(lambda *refs: update_kernel(count, *refs), grid_spec=pltpu...  6.53 us
  transfers between devices with their start and end apart: 39, of which 24 were waited for; matrix products, arithmetic and copies ran while one was open for 5% of the time, Pallas kernels for 14%

profile of v2, /device:TPU:16, one launch (start us, length us, event | category | flops | bytes accessed | tf_op | source)
XLA Modules:
  0.0 199.2 jit_solution(10837934256017494592)
XLA Ops:
  7.3 1.1 convert_element_type.53
  8.4 1.4 collective-permute-start.2
  9.7 1.4 collective-permute-start
  11.1 1.5 collective-permute-start.1
  12.6 1.3 constant_dynamic-slice_fusion
  13.9 2.6 %collective-permute-done = bf16[128,512]{1,0:T(8,128)(2,1)S(1)} collective-permute-done((bf16[128,512]{1,0:T(8,128)(2,1)S(1)}, bf16[128,512]{1,0:T(8,128)(2,1)S(1)}, u32[]{:S(2)}, u32[]{:S(2)}) %collective-permute-start) | collective-permute-done | bytes 131104 | tf_op jit(solution)/shard_map/ppermute | solution.py:36
  16.4 1.1 collective-permute-done.1
  17.7 2.0 collective-permute-start.5
  19.6 4.0 %collective-permute-start.4 = (bf16[512,512]{1,0:T(8,128)(2,1)S(1)}, bf16[512,512]{1,0:T(8,128)(2,1)}, u32[]{:S(2)}, u32[]{:S(2)}) collective-permute-start(bf16[512,512]{1,0:T(8,128)(2,1)S(1)} %pad_maximum_fusion.refs_2_), channel_id=1, source_target_pairs={{0,224},{8,232},{16,240},{24,248},{32,0},{40,8},{48,16},{56,24},{6... | collective-permute-start | bytes 1572872 | tf_op jit(solution)/shard_map/ppermute | solution.py:32
  23.7 1.9 collective-permute-start.3
  25.6 8.0 %collective-permute-done.5.refs_4_ = bf16[512,512]{1,0:T(8,128)(2,1)} collective-permute-done((bf16[512,512]{1,0:T(8,128)(2,1)S(1)}, bf16[512,512]{1,0:T(8,128)(2,1)}, u32[]{:S(2)}, u32[]{:S(2)}) %collective-permute-start.5) | collective-permute-done | bytes 524320 | tf_op jit(solution)/shard_map/ppermute | solution.py:32
  33.6 2.7 %collective-permute-done.3 = bf16[64,4096]{1,0:T(8,128)(2,1)S(1)} collective-permute-done((bf16[64,4096]{1,0:T(8,128)(2,1)S(1)}, bf16[64,4096]{1,0:T(8,128)(2,1)S(1)}, u32[]{:S(2)}, u32[]{:S(2)}) %collective-permute-start.3) | collective-permute-done | bytes 524320 | tf_op jit(solution)/shard_map/ppermute | solution.py:36
  36.3 0.8 copy-done.8
  37.2 4.6 %multiply_reduce_fusion = f32[512]{0:T(512)S(1)} fusion(bf16[512,4096]{1,0:T(8,128)(2,1)} %refs_2_.5, bf16[512,4096]{1,0:T(8,128)(2,1)} %refs_1_.8), kind=kLoop, calls=%fused_computation | loop fusion | flops 8388096 | bytes 8390656 | tf_op jit(solution)/shard_map/reduce_sum | solution.py:309
  42.3 2.3 %collective-permute-start.9 = (f32[4,128]{1,0:T(4,128)S(1)}, f32[4,128]{1,0:T(4,128)S(1)}, u32[]{:S(2)}, u32[]{:S(2)}) collective-permute-start(f32[4,128]{1,0:T(4,128)S(1)} %multiply_bitcast_fusion), channel_id=1, source_target_pairs={{0,8},{8,0},{16,24},{24,16},{32,40},{40,32},{48,56},{56,48},{64,72... | collective-permute-start | bytes 6152 | tf_op jit(solution)/shard_map/ppermute | solution.py:36
  44.7 1.7 collective-permute-start.6
  46.7 0.6 pad_maximum_fusion.3.refs_8_
  47.3 1.6 collective-permute-start.12
  48.9 9.8 %collective-permute-done.7.refs_3_.refs_6_ = bf16[512,512]{1,0:T(8,128)(2,1)} collective-permute-done((bf16[512,512]{1,0:T(8,128)(2,1)}, bf16[512,512]{1,0:T(8,128)(2,1)}, u32[]{:S(2)}, u32[]{:S(2)}) %collective-permute-start.7) | collective-permute-done | bytes 524320 | tf_op jit(solution)/shard_map/ppermute | solution.py:32
  58.7 6.3 %collective-permute-done.8.right_3 = bf16[512,1024]{1,0:T(8,128)(2,1)S(1)} collective-permute-done((bf16[512,1024]{1,0:T(8,128)(2,1)}, bf16[512,1024]{1,0:T(8,128)(2,1)S(1)}, u32[]{:S(2)}, u32[]{:S(2)}) %collective-permute-start.8) | collective-permute-done | bytes 1048608 | tf_op jit(solution)/shard_map/ppermute | solution.py:36
  65.1 1.5 collective-permute-start.10
  67.7 4.5 %shard_map.93.refs_4_ = f32[512,512]{1,0:T(8,128)} custom-call(s32[3]{0:T(128)} %pad_add_fusion.refs_0_.place, bf16[512,4096]{1,0:T(8,128)(2,1)} %refs_1_.8, bf16[512,512]{1,0:T(8,128)(2,1)} %copy-done.5, bf16[512,512]{1,0:T(8,128)(2,1)} %collective-permute-done.4.refs_3_, bf16[512,512]{1,0:T(8,128)(2,1)} %collective-permute-done.5.refs_4_), custom_call_target="tpu_custom_call" | custom-call | flops 805306368 | bytes 5242880 | tf_op jit(solution)/shard_map/pallas_call | solution.py:93
  72.2 4.5 %shard_map.94.refs_6_ = f32[512,512]{1,0:T(8,128)} custom-call(s32[3]{0:T(128)} %pad_add_fusion.refs_0_.place, bf16[512,4096]{1,0:T(8,128)(2,1)} %refs_1_.8, bf16[512,512]{1,0:T(8,128)(2,1)} %copy-done.7, bf16[512,512]{1,0:T(8,128)(2,1)} %collective-permute-done.7.refs_3_.refs_6_, f32[512,512]{1,0:T(8,128)} %shard_map.93.refs_4_), custom_call_target="tpu_custom_call" | custom-call | flops 536870912 | bytes 4194304 | tf_op jit(solution)/shard_map/pallas_call | solution.py:93
  76.7 1.8 collective-permute-done.11.refs_4_
  78.5 1.3 collective-permute-start.13
  80.5 3.2 %collective-permute-start.26 = (bf16[64,1024]{1,0:T(8,128)(2,1)S(1)}, bf16[64,1024]{1,0:T(8,128)(2,1)S(1)}, u32[]{:S(2)}, u32[]{:S(2)}) collective-permute-start(bf16[64,1024]{1,0:T(8,128)(2,1)S(1)} %get-tuple-element.46), channel_id=1, source_target_pairs={{0,8},{8,0},{16,24},{24,16},{32,40},{40,32},{48,56},{56,48},{64,72... | collective-permute-start | bytes 393224 | tf_op jit(solution)/shard_map/ppermute | solution.py:36
  83.7 1.6 collective-permute-start.28
  85.3 1.4 collective-permute-done.26
  86.7 3.5 %collective-permute-done.27 = bf16[64,1024]{1,0:T(8,128)(2,1)S(1)} collective-permute-done((bf16[64,1024]{1,0:T(8,128)(2,1)S(1)}, bf16[64,1024]{1,0:T(8,128)(2,1)S(1)}, u32[]{:S(2)}, u32[]{:S(2)}) %collective-permute-start.27) | collective-permute-done | bytes 131104 | tf_op jit(solution)/shard_map/ppermute | solution.py:36
  90.2 0.8 pad_maximum_fusion.1
  91.0 3.3 %collective-permute-start.18 = (bf16[512,1024]{1,0:T(8,128)(2,1)}, bf16[512,1024]{1,0:T(8,128)(2,1)S(1)}, u32[]{:S(2)}, u32[]{:S(2)}) collective-permute-start(bf16[512,1024]{1,0:T(8,128)(2,1)} %right.1), channel_id=1, source_target_pairs={{0,16},{8,24},{16,0},{24,8},{32,48},{40,56},{48,32},{56,40},{64,80... | collective-permute-start | bytes 3145736 | tf_op jit(solution)/shard_map/ppermute | solution.py:36
  94.3 0.7 dynamic_slice.28
  95.0 5.2 %shard_map.95.refs_7_ = f32[512,512]{1,0:T(8,128)} custom-call(s32[3]{0:T(128)} %pad_add_fusion.refs_0_.place, bf16[512,4096]{1,0:T(8,128)(2,1)} %all-gather.3.cloned.1.call-done.refs_1_.refs_2_, bf16[512,512]{1,0:T(8,128)(2,1)} %copy-done.5, bf16[512,512]{1,0:T(8,128)(2,1)} %collective-permute-done.4.refs_3_, ...), custom_call_target="tpu_custom_call" | custom-call | flops 1342177280 | bytes 7340032 | tf_op jit(solution)/shard_map/pallas_call | solution.py:93
  100.2 7.3 %shard_map.96 = f32[8,128]{1,0:T(8,128)} custom-call(s32[3]{0:T(128)} %pad_add_fusion.refs_0_.place, bf16[512,4096]{1,0:T(8,128)(2,1)} %refs_1_.8, bf16[512,4096]{1,0:T(8,128)(2,1)} %all-gather.3.cloned.1.call-done.refs_1_.refs_2_, bf16[512,512]{1,0:T(8,128)(2,1)} %collective-permute-done.10.refs_3_, bf16[512,512]{1,0:T(8,128)(2,1)} %collective-permute-done.11.refs_4_, ...), custom_call_target="tpu_custom_call" | custom-call | flops 1610612736 | bytes 6291456 | tf_op jit(solution)/shard_map/pallas_call | solution.py:149
  107.6 1.4 collective-permute-done.14
  109.0 0.7 add.123
  109.7 14.4 %collective-permute-start.17 = (f32[8,128]{1,0:T(8,128)S(1)}, f32[8,128]{1,0:T(8,128)S(1)}, u32[]{:S(2)}, u32[]{:S(2)}) collective-permute-start(f32[8,128]{1,0:T(8,128)S(1)} %add.123), channel_id=1, source_target_pairs={{0,6},{1,7},{2,4},{3,5},{4,2},{5,3},{6,0},{7,1},{8,14},{9,15},{10,... | collective-permute-start | bytes 12296 | tf_op jit(solution)/shard_map/ppermute | solution.py:40
  124.1 0.8 collective-permute-start.16
  124.9 0.8 collective-permute-done.17
  125.7 3.5 %collective-permute-done.16 = f32[8,128]{1,0:T(8,128)S(1)} collective-permute-done((f32[8,128]{1,0:T(8,128)S(1)}, f32[8,128]{1,0:T(8,128)S(1)}, u32[]{:S(2)}, u32[]{:S(2)}) %collective-permute-start.16) | collective-permute-done | bytes 4128 | tf_op jit(solution)/shard_map/ppermute | solution.py:40
  129.5 4.0 %collective-permute-start.19 = (f32[8,128]{1,0:T(8,128)S(1)}, f32[8,128]{1,0:T(8,128)S(1)}, u32[]{:S(2)}, u32[]{:S(2)}) collective-permute-start(f32[8,128]{1,0:T(8,128)S(1)} %pad_maximum_fusion.4), channel_id=1, source_target_pairs={{0,8},{8,0},{16,24},{24,16},{32,40},{40,32},{48,56},{56,48},{64,72... | collective-permute-start | bytes 12296 | tf_op jit(solution)/shard_map/ppermute | solution.py:36
  133.5 1.1 collective-permute-done.20
  135.3 2.4 %collective-permute-start.24 = (f32[8,128]{1,0:T(8,128)S(1)}, f32[8,128]{1,0:T(8,128)S(1)}, u32[]{:S(2)}, u32[]{:S(2)}) collective-permute-start(f32[8,128]{1,0:T(8,128)S(1)} %pad_maximum_fusion.5), channel_id=1, source_target_pairs={{0,64},{8,72},{16,80},{24,88},{32,96},{40,104},{48,112},{56,120},{... | collective-permute-start | bytes 12296 | tf_op jit(solution)/shard_map/ppermute | solution.py:32
  137.7 1.2 collective-permute-done.23
  138.8 2.2 %collective-permute-done.24 = f32[8,128]{1,0:T(8,128)S(1)} collective-permute-done((f32[8,128]{1,0:T(8,128)S(1)}, f32[8,128]{1,0:T(8,128)S(1)}, u32[]{:S(2)}, u32[]{:S(2)}) %collective-permute-start.24) | collective-permute-done | bytes 4128 | tf_op jit(solution)/shard_map/ppermute | solution.py:32
  141.0 1.5 collective-permute-done.22
  142.5 3.9 %collective-permute-start.25 = (f32[8,128]{1,0:T(8,128)S(1)}, f32[8,128]{1,0:T(8,128)S(1)}, u32[]{:S(2)}, u32[]{:S(2)}) collective-permute-start(f32[8,128]{1,0:T(8,128)S(1)} %add_add_fusion), channel_id=1, source_target_pairs={{0,128},{8,136},{16,144},{24,152},{32,160},{40,168},{48,176},{56,1... | collective-permute-start | bytes 12296 | tf_op jit(solution)/shard_map/ppermute | solution.py:32
  146.4 3.9 %collective-permute-done.25 = f32[8,128]{1,0:T(8,128)S(1)} collective-permute-done((f32[8,128]{1,0:T(8,128)S(1)}, f32[8,128]{1,0:T(8,128)S(1)}, u32[]{:S(2)}, u32[]{:S(2)}) %collective-permute-start.25) | collective-permute-done | bytes 4128 | tf_op jit(solution)/shard_map/ppermute | solution.py:32
  150.4 1.9 copy-done.1
  152.2 3.7 %shard_map.97 = (bf16[128,512]{1,0:T(8,128)(2,1)S(1)}, bf16[128,512]{1,0:T(8,128)(2,1)S(1)}, f32[4,128]{1,0:T(4,128)}, bf16[512,1024]{1,0:T(8,128)(2,1)S(1)}, bf16[1536,1024]{1,0:T(8,128)(2,1)S(1)}) custom-call(s32[3]{0:T(128)S(1)} %copy-done.4, f32[8,128]{1,0:T(8,128)S(1)} %add.141.sums, bf16[512,4096]{1,0:T(8,128)(2,1)} %refs_2_.5, ...), custom_call_target="tpu_custom_call" | custom-call | flops 536870912 | bytes 6291456 | tf_op jit(solution)/shard_map/pallas_call | solution.py:239
  156.5 2.8 %collective-permute-start.33 = (bf16[128,512]{1,0:T(8,128)(2,1)S(1)}, bf16[128,512]{1,0:T(8,128)(2,1)S(1)}, u32[]{:S(2)}, u32[]{:S(2)}) collective-permute-start(bf16[128,512]{1,0:T(8,128)(2,1)S(1)} %get-tuple-element.55), channel_id=1, source_target_pairs={{0,224},{8,232},{16,240},{24,248},{32,0},{40,8},{48,16},{56,24},{6... | collective-permute-start | bytes 393224 | tf_op jit(solution)/shard_map/ppermute | solution.py:32
  159.2 2.0 shard_map.100
  161.2 2.3 %collective-permute-done.29 = bf16[128,512]{1,0:T(8,128)(2,1)S(1)} collective-permute-done((bf16[128,512]{1,0:T(8,128)(2,1)S(1)}, bf16[128,512]{1,0:T(8,128)(2,1)S(1)}, u32[]{:S(2)}, u32[]{:S(2)}) %collective-permute-start.29) | collective-permute-done | bytes 131104 | tf_op jit(solution)/shard_map/ppermute | solution.py:32
  163.8 3.2 %collective-permute-start.34 = (bf16[128,1024]{1,0:T(8,128)(2,1)S(1)}, bf16[128,1024]{1,0:T(8,128)(2,1)S(1)}, u32[]{:S(2)}, u32[]{:S(2)}) collective-permute-start(bf16[128,1024]{1,0:T(8,128)(2,1)S(1)} %get-tuple-element.69), channel_id=1, source_target_pairs={{0,224},{8,232},{16,240},{24,248},{32,0},{40,8},{48,16},{56,24},{6... | collective-permute-start | bytes 786440 | tf_op jit(solution)/shard_map/ppermute | solution.py:32
  167.0 2.0 %shard_map.99 = f32[2,128,1024]{2,1,0:T(8,128)S(1)} custom-call(s32[3]{0:T(128)S(1)} %copy-done.4, bf16[512,4096]{1,0:T(8,128)(2,1)S(1)} %copy-done, bf16[512,4096]{1,0:T(8,128)(2,1)S(1)} %copy-done, bf16[1536,1024]{1,0:T(8,128)(2,1)S(1)} %copy-done.1, bf16[1536,1024]{1,0:T(8,128)(2,1)S(1)} %copy-done.1, ...), custom_call_target="tpu_custom_call" | custom-call | flops 536870912 | bytes 1048576 | tf_op jit(solution)/shard_map/pallas_call | solution.py:264
  169.0 4.3 %collective-permute-done.30 = bf16[128,1024]{1,0:T(8,128)(2,1)S(1)} collective-permute-done((bf16[128,1024]{1,0:T(8,128)(2,1)S(1)}, bf16[128,1024]{1,0:T(8,128)(2,1)S(1)}, u32[]{:S(2)}, u32[]{:S(2)}) %collective-permute-start.30) | collective-permute-done | bytes 262176 | tf_op jit(solution)/shard_map/ppermute | solution.py:32
  173.5 2.2 %collective-permute-start.31 = (bf16[128,1024]{1,0:T(8,128)(2,1)S(1)}, bf16[128,1024]{1,0:T(8,128)(2,1)S(1)}, u32[]{:S(2)}, u32[]{:S(2)}) collective-permute-start(bf16[128,1024]{1,0:T(8,128)(2,1)S(1)} %get-tuple-element.66), channel_id=1, source_target_pairs={{0,32},{8,40},{16,48},{24,56},{32,64},{40,72},{48,80},{56,88},{64,... | collective-permute-start | bytes 786440 | tf_op jit(solution)/shard_map/ppermute | solution.py:32
  175.6 1.2 collective-permute-start.35
  176.8 2.6 %shard_map.98 = f32[3,128,1024]{2,1,0:T(8,128)S(1)} custom-call(s32[3]{0:T(128)S(1)} %copy-done.4, bf16[512,4096]{1,0:T(8,128)(2,1)S(1)} %copy-done, bf16[512,4096]{1,0:T(8,128)(2,1)S(1)} %copy-done, bf16[512,4096]{1,0:T(8,128)(2,1)S(1)} %copy-done, bf16[1536,1024]{1,0:T(8,128)(2,1)S(1)} %copy-done.1, bf16[1536,1024]{1,0:T(8,128)(2,1)S(1)} %copy-done.1, ...), custom_call_target="tpu_custom_call" | custom-call | flops 536870912 | bytes 1048576 | tf_op jit(solution)/shard_map/pallas_call | solution.py:264
  179.3 3.5 %collective-permute-done.31 = bf16[128,1024]{1,0:T(8,128)(2,1)S(1)} collective-permute-done((bf16[128,1024]{1,0:T(8,128)(2,1)S(1)}, bf16[128,1024]{1,0:T(8,128)(2,1)S(1)}, u32[]{:S(2)}, u32[]{:S(2)}) %collective-permute-start.31) | collective-permute-done | bytes 262176 | tf_op jit(solution)/shard_map/ppermute | solution.py:32
  183.0 1.7 collective-permute-start.32
  184.7 1.6 collective-permute-start.36
  186.4 4.3 %collective-permute-done.32 = bf16[128,1024]{1,0:T(8,128)(2,1)S(1)} collective-permute-done((bf16[128,1024]{1,0:T(8,128)(2,1)S(1)}, bf16[128,1024]{1,0:T(8,128)(2,1)S(1)}, u32[]{:S(2)}, u32[]{:S(2)}) %collective-permute-start.32) | collective-permute-done | bytes 262176 | tf_op jit(solution)/shard_map/ppermute | solution.py:32
  191.1 1.2 fusion.14
  (75 shorter events, 5.5 us)
Async XLA Ops:
  7.2 83.8 %all-gather.3.cloned.1.call-start = ((), (), s32[]{:S(2)}) async-start(), calls=%async_computation | async-start | bytes 4718592 | tf_op jit(solution)/shard_map/all_gather | solution.py:302
  8.4 5.5 %collective-permute-start.2 = (bf16[128,512]{1,0:T(8,128)(2,1)S(1)}, bf16[128,512]{1,0:T(8,128)(2,1)S(1)}, u32[]{:S(2)}, u32[]{:S(2)}) collective-permute-start(bf16[128,512]{1,0:T(8,128)(2,1)S(1)} %get-tuple-element.77), channel_id=1, source_target_pairs={{0,8},{8,0},{16,24},{24,16},{32,40},{40,32},{48,56},{56,48},{64,72... | collective-permute-start | bytes 393224 | tf_op jit(solution)/shard_map/ppermute | solution.py:36
  9.7 6.7 %collective-permute-start = (bf16[128,512]{1,0:T(8,128)(2,1)S(1)}, bf16[128,512]{1,0:T(8,128)(2,1)S(1)}, u32[]{:S(2)}, u32[]{:S(2)}) collective-permute-start(bf16[128,512]{1,0:T(8,128)(2,1)S(1)} %get-tuple-element.77), channel_id=1, source_target_pairs={{0,24},{8,16},{16,8},{24,0},{32,56},{40,48},{48,40},{56,32},{64,88... | collective-permute-start | bytes 393224 | tf_op jit(solution)/shard_map/ppermute | solution.py:36
  11.1 6.5 %collective-permute-start.1 = (bf16[128,512]{1,0:T(8,128)(2,1)S(1)}, bf16[128,512]{1,0:T(8,128)(2,1)S(1)}, u32[]{:S(2)}, u32[]{:S(2)}) collective-permute-start(bf16[128,512]{1,0:T(8,128)(2,1)S(1)} %get-tuple-element.78), channel_id=1, source_target_pairs={{0,16},{8,24},{16,0},{24,8},{32,48},{40,56},{48,32},{56,40},{64,80... | collective-permute-start | bytes 393224 | tf_op jit(solution)/shard_map/ppermute | solution.py:36
  17.7 24.1 %copy-start.5 = (bf16[512,512]{1,0:T(8,128)(2,1)}, bf16[512,512]{1,0:T(8,128)(2,1)S(1)}, u32[]{:S(2)}) copy-start(bf16[512,512]{1,0:T(8,128)(2,1)S(1)} %pad_maximum_fusion.refs_2_) | copy-start | bytes 1572868
  17.7 15.9 %collective-permute-start.5 = (bf16[512,512]{1,0:T(8,128)(2,1)S(1)}, bf16[512,512]{1,0:T(8,128)(2,1)}, u32[]{:S(2)}, u32[]{:S(2)}) collective-permute-start(bf16[512,512]{1,0:T(8,128)(2,1)S(1)} %pad_maximum_fusion.refs_2_), channel_id=1, source_target_pairs={{0,32},{8,40},{16,48},{24,56},{32,64},{40,72},{48,80},{56,88},{64,... | collective-permute-start | bytes 1572872 | tf_op jit(solution)/shard_map/ppermute | solution.py:32
  19.6 13.9 %collective-permute-start.4 = (bf16[512,512]{1,0:T(8,128)(2,1)S(1)}, bf16[512,512]{1,0:T(8,128)(2,1)}, u32[]{:S(2)}, u32[]{:S(2)}) collective-permute-start(bf16[512,512]{1,0:T(8,128)(2,1)S(1)} %pad_maximum_fusion.refs_2_), channel_id=1, source_target_pairs={{0,224},{8,232},{16,240},{24,248},{32,0},{40,8},{48,16},{56,24},{6... | collective-permute-start | bytes 1572872 | tf_op jit(solution)/shard_map/ppermute | solution.py:32
  23.7 12.6 %collective-permute-start.3 = (bf16[64,4096]{1,0:T(8,128)(2,1)S(1)}, bf16[64,4096]{1,0:T(8,128)(2,1)S(1)}, u32[]{:S(2)}, u32[]{:S(2)}) collective-permute-start(bf16[64,4096]{1,0:T(8,128)(2,1)S(1)} %get-tuple-element.30), channel_id=1, source_target_pairs={{0,8},{8,0},{16,24},{24,16},{32,40},{40,32},{48,56},{56,48},{64,72... | collective-permute-start | bytes 1572872 | tf_op jit(solution)/shard_map/ppermute | solution.py:36
  36.3 0.8 copy-start.8
  37.1 113.2 %all-gather.5.cloned.1.call-start = ((), (), s32[]{:S(2)}) async-start(), calls=%async_computation.1 | async-start | bytes 3538944 | tf_op jit(solution)/shard_map/all_gather | solution.py:334
  41.8 23.2 %collective-permute-start.8 = (bf16[512,1024]{1,0:T(8,128)(2,1)}, bf16[512,1024]{1,0:T(8,128)(2,1)S(1)}, u32[]{:S(2)}, u32[]{:S(2)}) collective-permute-start(bf16[512,1024]{1,0:T(8,128)(2,1)} %right.1), channel_id=1, source_target_pairs={{0,24},{8,16},{16,8},{24,0},{32,56},{40,48},{48,40},{56,32},{64,88... | collective-permute-start | bytes 3145736 | tf_op jit(solution)/shard_map/ppermute | solution.py:36
  42.3 4.4 %collective-permute-start.9 = (f32[4,128]{1,0:T(4,128)S(1)}, f32[4,128]{1,0:T(4,128)S(1)}, u32[]{:S(2)}, u32[]{:S(2)}) collective-permute-start(f32[4,128]{1,0:T(4,128)S(1)} %multiply_bitcast_fusion), channel_id=1, source_target_pairs={{0,8},{8,0},{16,24},{24,16},{32,40},{40,32},{48,56},{56,48},{64,72... | collective-permute-start | bytes 6152 | tf_op jit(solution)/shard_map/ppermute | solution.py:36
  44.7 14.0 %collective-permute-start.6 = (bf16[512,512]{1,0:T(8,128)(2,1)}, bf16[512,512]{1,0:T(8,128)(2,1)S(1)}, u32[]{:S(2)}, u32[]{:S(2)}) collective-permute-start(bf16[512,512]{1,0:T(8,128)(2,1)} %collective-permute-done.4.refs_3_), channel_id=1, source_target_pairs={{0,224},{8,232},{16,240},{24,248},{32,0},{40,8},{48,16},{56,24},{6... | collective-permute-start | bytes 1572872 | tf_op jit(solution)/shard_map/ppermute | solution.py:32
  46.3 12.4 %collective-permute-start.7 = (bf16[512,512]{1,0:T(8,128)(2,1)}, bf16[512,512]{1,0:T(8,128)(2,1)}, u32[]{:S(2)}, u32[]{:S(2)}) collective-permute-start(bf16[512,512]{1,0:T(8,128)(2,1)} %collective-permute-done.5.refs_4_), channel_id=1, source_target_pairs={{0,32},{8,40},{16,48},{24,56},{32,64},{40,72},{48,80},{56,88},{64,... | collective-permute-start | bytes 1572872 | tf_op jit(solution)/shard_map/ppermute | solution.py:32
  47.3 31.2 %collective-permute-start.12 = (bf16[512,1024]{1,0:T(8,128)(2,1)}, bf16[512,1024]{1,0:T(8,128)(2,1)S(1)}, u32[]{:S(2)}, u32[]{:S(2)}) collective-permute-start(bf16[512,1024]{1,0:T(8,128)(2,1)} %right.1), channel_id=1, source_target_pairs={{0,8},{8,0},{16,24},{24,16},{32,40},{40,32},{48,56},{56,48},{64,72... | collective-permute-start | bytes 3145736 | tf_op jit(solution)/shard_map/ppermute | solution.py:36
  58.7 13.5 %copy-start.7 = (bf16[512,512]{1,0:T(8,128)(2,1)}, bf16[512,512]{1,0:T(8,128)(2,1)S(1)}, u32[]{:S(2)}) copy-start(bf16[512,512]{1,0:T(8,128)(2,1)S(1)} %collective-permute-done.6.refs_2_.refs_5_) | copy-start | bytes 1572868
  65.1 11.7 %collective-permute-start.10 = (bf16[512,512]{1,0:T(8,128)(2,1)S(1)}, bf16[512,512]{1,0:T(8,128)(2,1)}, u32[]{:S(2)}, u32[]{:S(2)}) collective-permute-start(bf16[512,512]{1,0:T(8,128)(2,1)S(1)} %collective-permute-done.6.refs_2_.refs_5_), channel_id=1, source_target_pairs={{0,224},{8,232},{16,240},{24,248},{32,0},{40,8},{48,16},{56,24},{6... | collective-permute-start | bytes 1572872 | tf_op jit(solution)/shard_map/ppermute | solution.py:32
  66.5 12.0 %collective-permute-start.11 = (bf16[512,512]{1,0:T(8,128)(2,1)}, bf16[512,512]{1,0:T(8,128)(2,1)}, u32[]{:S(2)}, u32[]{:S(2)}) collective-permute-start(bf16[512,512]{1,0:T(8,128)(2,1)} %collective-permute-done.7.refs_3_.refs_6_), channel_id=1, source_target_pairs={{0,32},{8,40},{16,48},{24,56},{32,64},{40,72},{48,80},{56,88},{64,... | collective-permute-start | bytes 1572872 | tf_op jit(solution)/shard_map/ppermute | solution.py:32
  76.7 17.6 %copy-start.10 = (f32[1024]{0:T(1024)S(1)}, f32[1024]{0:T(1024)}, u32[]{:S(2)}) copy-start(f32[1024]{0:T(1024)} %param.9) | copy-start | bytes 12292
  78.5 21.7 %copy-start.2 = (bf16[512,1024]{1,0:T(8,128)(2,1)}, bf16[512,1024]{1,0:T(8,128)(2,1)S(1)}, u32[]{:S(2)}) copy-start(bf16[512,1024]{1,0:T(8,128)(2,1)S(1)} %collective-permute-done.12.refs_10_.right_1) | copy-start | bytes 3145732
  78.5 12.5 %collective-permute-start.13 = (bf16[512,512]{1,0:T(8,128)(2,1)}, bf16[512,512]{1,0:T(8,128)(2,1)}, u32[]{:S(2)}, u32[]{:S(2)}) collective-permute-start(bf16[512,512]{1,0:T(8,128)(2,1)} %collective-permute-done.10.refs_3_), channel_id=1, source_target_pairs={{0,224},{8,232},{16,240},{24,248},{32,0},{40,8},{48,16},{56,24},{6... | collective-permute-start | bytes 1572872 | tf_op jit(solution)/shard_map/ppermute | solution.py:32
  80.5 6.1 %collective-permute-start.26 = (bf16[64,1024]{1,0:T(8,128)(2,1)S(1)}, bf16[64,1024]{1,0:T(8,128)(2,1)S(1)}, u32[]{:S(2)}, u32[]{:S(2)}) collective-permute-start(bf16[64,1024]{1,0:T(8,128)(2,1)S(1)} %get-tuple-element.46), channel_id=1, source_target_pairs={{0,8},{8,0},{16,24},{24,16},{32,40},{40,32},{48,56},{56,48},{64,72... | collective-permute-start | bytes 393224 | tf_op jit(solution)/shard_map/ppermute | solution.py:36
  83.7 6.5 %collective-permute-start.27 = (bf16[64,1024]{1,0:T(8,128)(2,1)S(1)}, bf16[64,1024]{1,0:T(8,128)(2,1)S(1)}, u32[]{:S(2)}, u32[]{:S(2)}) collective-permute-start(bf16[64,1024]{1,0:T(8,128)(2,1)S(1)} %get-tuple-element.47), channel_id=1, source_target_pairs={{0,16},{8,24},{16,0},{24,8},{32,48},{40,56},{48,32},{56,40},{64,80... | collective-permute-start | bytes 393224 | tf_op jit(solution)/shard_map/ppermute | solution.py:36
  83.7 6.5 %collective-permute-start.28 = (bf16[64,1024]{1,0:T(8,128)(2,1)S(1)}, bf16[64,1024]{1,0:T(8,128)(2,1)S(1)}, u32[]{:S(2)}, u32[]{:S(2)}) collective-permute-start(bf16[64,1024]{1,0:T(8,128)(2,1)S(1)} %get-tuple-element.48), channel_id=1, source_target_pairs={{0,24},{8,16},{16,8},{24,0},{32,56},{40,48},{48,40},{56,32},{64,88... | collective-permute-start | bytes 393224 | tf_op jit(solution)/shard_map/ppermute | solution.py:36
  91.0 38.3 %collective-permute-start.18 = (bf16[512,1024]{1,0:T(8,128)(2,1)}, bf16[512,1024]{1,0:T(8,128)(2,1)S(1)}, u32[]{:S(2)}, u32[]{:S(2)}) collective-permute-start(bf16[512,1024]{1,0:T(8,128)(2,1)} %right.1), channel_id=1, source_target_pairs={{0,16},{8,24},{16,0},{24,8},{32,48},{40,56},{48,32},{56,40},{64,80... | collective-permute-start | bytes 3145736 | tf_op jit(solution)/shard_map/ppermute | solution.py:36
  100.2 29.1 %copy-start.9 = (s32[512]{0:T(512)S(1)}, s32[512]{0:T(512)}, u32[]{:S(2)}) copy-start(s32[512]{0:T(512)} %param.10) | copy-start | bytes 6148
  100.2 50.1 %copy-start.3 = (bf16[512,1024]{1,0:T(8,128)(2,1)S(1)}, bf16[512,1024]{1,0:T(8,128)(2,1)}, u32[]{:S(2)}) copy-start(bf16[512,1024]{1,0:T(8,128)(2,1)} %copy-done.2) | copy-start | bytes 3145732
  100.2 50.1 %copy-start.4 = (s32[3]{0:T(128)S(1)}, s32[3]{0:T(128)}, u32[]{:S(2)}) copy-start(s32[3]{0:T(128)} %pad_add_fusion.refs_0_.place) | copy-start | bytes 40
  107.5 1.5 collective-permute-start.14
  109.7 16.0 %collective-permute-start.17 = (f32[8,128]{1,0:T(8,128)S(1)}, f32[8,128]{1,0:T(8,128)S(1)}, u32[]{:S(2)}, u32[]{:S(2)}) collective-permute-start(f32[8,128]{1,0:T(8,128)S(1)} %add.123), channel_id=1, source_target_pairs={{0,6},{1,7},{2,4},{3,5},{4,2},{5,3},{6,0},{7,1},{8,14},{9,15},{10,... | collective-permute-start | bytes 12296 | tf_op jit(solution)/shard_map/ppermute | solution.py:40
  124.1 5.2 %collective-permute-start.16 = (f32[8,128]{1,0:T(8,128)S(1)}, f32[8,128]{1,0:T(8,128)S(1)}, u32[]{:S(2)}, u32[]{:S(2)}) collective-permute-start(f32[8,128]{1,0:T(8,128)S(1)} %add.123), channel_id=1, source_target_pairs={{0,4},{1,5},{2,6},{3,7},{4,0},{5,1},{6,2},{7,3},{8,12},{9,13},{10,... | collective-permute-start | bytes 12296 | tf_op jit(solution)/shard_map/ppermute | solution.py:40
  124.9 4.4 %collective-permute-start.15 = (f32[8,128]{1,0:T(8,128)S(1)}, f32[8,128]{1,0:T(8,128)S(1)}, u32[]{:S(2)}, u32[]{:S(2)}) collective-permute-start(f32[8,128]{1,0:T(8,128)S(1)} %add.123), channel_id=1, source_target_pairs={{0,2},{1,3},{2,0},{3,1},{4,6},{5,7},{6,4},{7,5},{8,10},{9,11},{10,... | collective-permute-start | bytes 12296 | tf_op jit(solution)/shard_map/ppermute | solution.py:40
  129.3 4.2 %collective-permute-start.21 = (f32[8,128]{1,0:T(8,128)S(1)}, f32[8,128]{1,0:T(8,128)S(1)}, u32[]{:S(2)}, u32[]{:S(2)}) collective-permute-start(f32[8,128]{1,0:T(8,128)S(1)} %pad_maximum_fusion.4), channel_id=1, source_target_pairs={{0,24},{8,16},{16,8},{24,0},{32,56},{40,48},{48,40},{56,32},{64,88... | collective-permute-start | bytes 12296 | tf_op jit(solution)/shard_map/ppermute | solution.py:36
  129.4 5.2 %collective-permute-start.20 = (f32[8,128]{1,0:T(8,128)S(1)}, f32[8,128]{1,0:T(8,128)S(1)}, u32[]{:S(2)}, u32[]{:S(2)}) collective-permute-start(f32[8,128]{1,0:T(8,128)S(1)} %pad_maximum_fusion.4), channel_id=1, source_target_pairs={{0,16},{8,24},{16,0},{24,8},{32,48},{40,56},{48,32},{56,40},{64,80... | collective-permute-start | bytes 12296 | tf_op jit(solution)/shard_map/ppermute | solution.py:36
  129.5 5.6 %collective-permute-start.19 = (f32[8,128]{1,0:T(8,128)S(1)}, f32[8,128]{1,0:T(8,128)S(1)}, u32[]{:S(2)}, u32[]{:S(2)}) collective-permute-start(f32[8,128]{1,0:T(8,128)S(1)} %pad_maximum_fusion.4), channel_id=1, source_target_pairs={{0,8},{8,0},{16,24},{24,16},{32,40},{40,32},{48,56},{56,48},{64,72... | collective-permute-start | bytes 12296 | tf_op jit(solution)/shard_map/ppermute | solution.py:36
  135.2 3.7 %collective-permute-start.23 = (f32[8,128]{1,0:T(8,128)S(1)}, f32[8,128]{1,0:T(8,128)S(1)}, u32[]{:S(2)}, u32[]{:S(2)}) collective-permute-start(f32[8,128]{1,0:T(8,128)S(1)} %pad_maximum_fusion.5), channel_id=1, source_target_pairs={{0,224},{8,232},{16,240},{24,248},{32,0},{40,8},{48,16},{56,24},{6... | collective-permute-start | bytes 12296 | tf_op jit(solution)/shard_map/ppermute | solution.py:32
  135.3 5.8 %collective-permute-start.24 = (f32[8,128]{1,0:T(8,128)S(1)}, f32[8,128]{1,0:T(8,128)S(1)}, u32[]{:S(2)}, u32[]{:S(2)}) collective-permute-start(f32[8,128]{1,0:T(8,128)S(1)} %pad_maximum_fusion.5), channel_id=1, source_target_pairs={{0,64},{8,72},{16,80},{24,88},{32,96},{40,104},{48,112},{56,120},{... | collective-permute-start | bytes 12296 | tf_op jit(solution)/shard_map/ppermute | solution.py:32
  137.7 4.8 %collective-permute-start.22 = (f32[8,128]{1,0:T(8,128)S(1)}, f32[8,128]{1,0:T(8,128)S(1)}, u32[]{:S(2)}, u32[]{:S(2)}) collective-permute-start(f32[8,128]{1,0:T(8,128)S(1)} %pad_maximum_fusion.5), channel_id=1, source_target_pairs={{0,32},{8,40},{16,48},{24,56},{32,64},{40,72},{48,80},{56,88},{64,... | collective-permute-start | bytes 12296 | tf_op jit(solution)/shard_map/ppermute | solution.py:32
  142.5 7.8 %collective-permute-start.25 = (f32[8,128]{1,0:T(8,128)S(1)}, f32[8,128]{1,0:T(8,128)S(1)}, u32[]{:S(2)}, u32[]{:S(2)}) collective-permute-start(f32[8,128]{1,0:T(8,128)S(1)} %add_add_fusion), channel_id=1, source_target_pairs={{0,128},{8,136},{16,144},{24,152},{32,160},{40,168},{48,176},{56,1... | collective-permute-start | bytes 12296 | tf_op jit(solution)/shard_map/ppermute | solution.py:32
  150.4 1.9 copy-start.1
  152.2 7.0 %copy-start = (bf16[512,4096]{1,0:T(8,128)(2,1)S(1)}, bf16[512,4096]{1,0:T(8,128)(2,1)}, u32[]{:S(2)}) copy-start(bf16[512,4096]{1,0:T(8,128)(2,1)} %refs_2_.5) | copy-start | bytes 12582916
  155.9 7.7 %collective-permute-start.29 = (bf16[128,512]{1,0:T(8,128)(2,1)S(1)}, bf16[128,512]{1,0:T(8,128)(2,1)S(1)}, u32[]{:S(2)}, u32[]{:S(2)}) collective-permute-start(bf16[128,512]{1,0:T(8,128)(2,1)S(1)} %get-tuple-element.54), channel_id=1, source_target_pairs={{0,32},{8,40},{16,48},{24,56},{32,64},{40,72},{48,80},{56,88},{64,... | collective-permute-start | bytes 393224 | tf_op jit(solution)/shard_map/ppermute | solution.py:32
  156.5 7.1 %collective-permute-start.33 = (bf16[128,512]{1,0:T(8,128)(2,1)S(1)}, bf16[128,512]{1,0:T(8,128)(2,1)S(1)}, u32[]{:S(2)}, u32[]{:S(2)}) collective-permute-start(bf16[128,512]{1,0:T(8,128)(2,1)S(1)} %get-tuple-element.55), channel_id=1, source_target_pairs={{0,224},{8,232},{16,240},{24,248},{32,0},{40,8},{48,16},{56,24},{6... | collective-permute-start | bytes 393224 | tf_op jit(solution)/shard_map/ppermute | solution.py:32
  163.7 9.6 %collective-permute-start.30 = (bf16[128,1024]{1,0:T(8,128)(2,1)S(1)}, bf16[128,1024]{1,0:T(8,128)(2,1)S(1)}, u32[]{:S(2)}, u32[]{:S(2)}) collective-permute-start(bf16[128,1024]{1,0:T(8,128)(2,1)S(1)} %get-tuple-element.68), channel_id=1, source_target_pairs={{0,32},{8,40},{16,48},{24,56},{32,64},{40,72},{48,80},{56,88},{64,... | collective-permute-start | bytes 786440 | tf_op jit(solution)/shard_map/ppermute | solution.py:32
  163.8 9.5 %collective-permute-start.34 = (bf16[128,1024]{1,0:T(8,128)(2,1)S(1)}, bf16[128,1024]{1,0:T(8,128)(2,1)S(1)}, u32[]{:S(2)}, u32[]{:S(2)}) collective-permute-start(bf16[128,1024]{1,0:T(8,128)(2,1)S(1)} %get-tuple-element.69), channel_id=1, source_target_pairs={{0,224},{8,232},{16,240},{24,248},{32,0},{40,8},{48,16},{56,24},{6... | collective-permute-start | bytes 786440 | tf_op jit(solution)/shard_map/ppermute | solution.py:32
  173.5 9.3 %collective-permute-start.31 = (bf16[128,1024]{1,0:T(8,128)(2,1)S(1)}, bf16[128,1024]{1,0:T(8,128)(2,1)S(1)}, u32[]{:S(2)}, u32[]{:S(2)}) collective-permute-start(bf16[128,1024]{1,0:T(8,128)(2,1)S(1)} %get-tuple-element.66), channel_id=1, source_target_pairs={{0,32},{8,40},{16,48},{24,56},{32,64},{40,72},{48,80},{56,88},{64,... | collective-permute-start | bytes 786440 | tf_op jit(solution)/shard_map/ppermute | solution.py:32
  175.6 15.5 %copy-start.6 = (f32[128,1024]{1,0:T(8,128)S(1)}, f32[128,1024]{1,0:T(8,128)}, u32[]{:S(2)}) copy-start(f32[128,1024]{1,0:T(8,128)} %param.11) | copy-start | bytes 1572868
  175.6 7.3 %collective-permute-start.35 = (bf16[128,1024]{1,0:T(8,128)(2,1)S(1)}, bf16[128,1024]{1,0:T(8,128)(2,1)S(1)}, u32[]{:S(2)}, u32[]{:S(2)}) collective-permute-start(bf16[128,1024]{1,0:T(8,128)(2,1)S(1)} %get-tuple-element.67), channel_id=1, source_target_pairs={{0,224},{8,232},{16,240},{24,248},{32,0},{40,8},{48,16},{56,24},{6... | collective-permute-start | bytes 786440 | tf_op jit(solution)/shard_map/ppermute | solution.py:32
  183.0 7.7 %collective-permute-start.32 = (bf16[128,1024]{1,0:T(8,128)(2,1)S(1)}, bf16[128,1024]{1,0:T(8,128)(2,1)S(1)}, u32[]{:S(2)}, u32[]{:S(2)}) collective-permute-start(bf16[128,1024]{1,0:T(8,128)(2,1)S(1)} %get-tuple-element.64), channel_id=1, source_target_pairs={{0,32},{8,40},{16,48},{24,56},{32,64},{40,72},{48,80},{56,88},{64,... | collective-permute-start | bytes 786440 | tf_op jit(solution)/shard_map/ppermute | solution.py:32
  184.7 6.4 %collective-permute-start.36 = (bf16[128,1024]{1,0:T(8,128)(2,1)S(1)}, bf16[128,1024]{1,0:T(8,128)(2,1)S(1)}, u32[]{:S(2)}, u32[]{:S(2)}) collective-permute-start(bf16[128,1024]{1,0:T(8,128)(2,1)S(1)} %get-tuple-element.65), channel_id=1, source_target_pairs={{0,224},{8,232},{16,240},{24,248},{32,0},{40,8},{48,16},{56,24},{6... | collective-permute-start | bytes 786440 | tf_op jit(solution)/shard_map/ppermute | solution.py:32
Sparse Core Ops, SparseCore 0:
  37.2 34.7 all-gather.2
  91.1 41.8 all-gather.4
